TPU v7x, 32 devices: a whole 2x2x4 slice. The times are simulated.
32 devices in a mesh: members: 2 (over x), tiles: 16 (over z, y, core).
Axes of the slice: x: 2, y: 2, z: 4, core: 2. Of those that a mesh axis runs over, the one named last changes fastest.
Arguments:
- atmos: float32 [60, 384, 1152], P('members', 'tiles'), parts along dimension 0, may hold values from -6 to 6
- water_anomaly: float32 [100, 128, 1440], P('members', 'tiles'), parts along dimension 0, may hold values from -6 to 6
- atm_flux: float32 [384, 2304], P('tiles', 'members'), parts along dimension 1, may hold values from -6 to 6
- ocean_mask: int32 [128, 1440], P('tiles'), may hold values from 0 to 1, as said below
- air_mixing_numbers: float32 [384, 1152], P('tiles'), may hold values from 0.02 to 0.24
- ocean_kappa: float32 [128, 1440], P('tiles'), may hold values from 0.02 to 0.24
- air_vertical_operator: float32 [30, 30], replicated, may hold values from -1.5 to 1.5
- ocean_column: float32 [50, 50], replicated, may hold values from -1.5 to 1.5
- a2o_source: int32 [16, 16, 48], P('tiles'), may hold values from 0 to 215
- a2o_target: int32 [16, 16, 48], P('tiles'), may hold values from 0 to 89, as said below
- a2o_count: int32 [16, 16], P('tiles'), may hold values from 0 to 48, as said below
- a2o_weight: float32 [16, 16, 48, 128], P('tiles'), may hold values from 0.2 to 0.8
- water_air_provider: int32 [16, 16, 48], P('tiles'), may hold values from 0 to 89
- water_air_receiver: int32 [16, 16, 48], P('tiles'), may hold values from 0 to 215, as said below
- water_air_live_tally: int32 [16, 16], P('tiles'), may hold values from 0 to 48, as said below
- water_air_overlay_share: float32 [16, 16, 48, 128], P('tiles'), may hold values from 0.2 to 0.8
Outputs:
- atmos_next: float32 [60, 384, 1152], P('members', 'tiles'), parts along dimension 0
- ocean_next: float32 [100, 128, 1440], P('members', 'tiles'), parts along dimension 0
- future_energy_exchange: float32 [384, 2304], P('tiles', 'members'), parts along dimension 1
There are 2 independent parts, one for each index of `members`. A program takes and returns all parts, laid end to end along the dimension named above; an argument that names none is the same for every part. Nothing has to cross between parts.
Inputs may be any that keep to these rules, and one draw needn't show every extreme that they name: `ocean_mask`: 1 marks sea; in each tile every block from some block number on is all land. `a2o_count`: with N the number of tiles, list the tile offsets 0, N - 1, N // 2 and then 1, 2, 3 and so on without repeats; tile d has live slots only from tiles d plus the first 5 of these offsets, modulo N. `a2o_target`: each destination block gets 2 live slots or none; blocks holding sea get 2. `water_air_live_tally`: with N the number of tiles, list the tile offsets 0, N - 1, N // 2 and then 1, 2, 3 and so on without repeats; tile d has live slots only from tiles d plus the first 10 of these offsets, modulo N. `water_air_receiver`: each destination block gets exactly 2 live slots.
All inputs are finite; a program needn't handle non-finite values.
Results may differ from a plain program's by a relative error of at most 0.0003.
Values sent between devices are 32-bit elements; how exact they have to be, the bound alone decides.
A program may use at most 128 MiB of HBM per device.

v0:
```python
import jax
import jax.numpy as jnp
from jax import lax
from jax.sharding import PartitionSpec as P

PATCH_SIZE = 128


AIR_EXCHANGER = 0.3
COUPLE_OCEAN = 0.5


def with_halo(cells, sides, width):
    for axis, dim in sides:
        count = lax.axis_size(axis)
        ends = count - 1
        head = lax.slice_in_dim(cells, 0, width, axis=dim)
        tail = lax.slice_in_dim(cells, cells.shape[dim] - width, cells.shape[dim], axis=dim)
        cells = jnp.concatenate(
            [
                lax.ppermute(tail, axis, [(i, (i + 1) % count) for i in range(ends)]),
                cells,
                lax.ppermute(head, axis, [((i + 1) % count, i) for i in range(ends)]),
            ],
            axis=dim,
        )
    return cells


def position_combination(values, target, count, weight, dest_count):
    slot_ids = jnp.arange(values.shape[1], dtype=jnp.int32)
    live = (slot_ids[None, :] < count[:, None]).astype(jnp.float32)
    terms = weight * values * live[:, :, None]
    block_ids = jnp.arange(dest_count, dtype=jnp.int32)
    onehot = (target[:, :, None] == block_ids).astype(jnp.float32)
    return jnp.einsum("scj,scb->jb", onehot, terms, precision=lax.Precision.HIGHEST)


def air_advance_interval(
    widened_array, mixing_coefficient, vertical_linear_system, skin_water_warmth
):
    interior_points = widened_array[:, 1:-1]
    beside = (
        widened_array[:, 2:]
        + widened_array[:, :-2]
        + jnp.roll(interior_points, 1, 2)
        + jnp.roll(interior_points, -1, 2)
    )
    mixed = jnp.einsum(
        "kl,lyx->kyx", vertical_linear_system, interior_points, precision=lax.Precision.HIGHEST
    )
    advanced_condition = (
        interior_points + mixing_coefficient * (beside - 4.0 * interior_points) + mixed
    )
    bottom_layer = advanced_condition[-1] + AIR_EXCHANGER * (
        skin_water_warmth - interior_points[-1]
    )
    return jnp.concatenate([advanced_condition[:-1], bottom_layer[None]], 0)


def ocean_advance(widened_array, mixing_coefficient, vertical_linear_system, water_entries, flux):
    interior_points = widened_array[:, 1:-1]
    beside = (
        widened_array[:, 2:]
        + widened_array[:, :-2]
        + jnp.roll(interior_points, 1, 2)
        + jnp.roll(interior_points, -1, 2)
    )
    mixed = jnp.einsum(
        "kl,lyx->kyx", vertical_linear_system, interior_points, precision=lax.Precision.HIGHEST
    )
    advanced_condition = interior_points + water_entries * (
        mixing_coefficient * (beside - 4.0 * interior_points) + mixed
    )
    surface = advanced_condition[0] + water_entries * COUPLE_OCEAN * flux
    return jnp.concatenate([surface[None], advanced_condition[1:]], 0)


def shards(
    atmos,
    water_anomaly,
    atm_flux,
    ocean_mask,
    air_mixing_numbers,
    ocean_kappa,
    air_vertical_operator,
    ocean_column,
    a2o_source,
    a2o_target,
    a2o_count,
    a2o_weight,
    water_air_provider,
    water_air_receiver,
    water_air_live_tally,
    water_air_overlay_share,
):
    water_entries = ocean_mask.astype(jnp.float32)
    skin_water_warmth = water_anomaly[0] * water_entries
    atmos_blocks = atm_flux.reshape(-1, PATCH_SIZE)
    water_patch_indices = skin_water_warmth.reshape(-1, PATCH_SIZE)
    atmosphere_destination_tile = atmos_blocks.shape[0]
    ocean_dest = water_patch_indices.shape[0]
    flux_list = a2o_source[0]
    warmth_entry_positions = water_air_provider[0]
    flux_send = atmos_blocks[flux_list]
    sent_water_warmth = water_patch_indices[warmth_entry_positions]
    received_energy_rate, received_water_warmth = (
        lax.all_to_all(flux_send, "tiles", split_axis=0, concat_axis=0, tiled=True),
        lax.all_to_all(sent_water_warmth, "tiles", split_axis=0, concat_axis=0, tiled=True),
    )
    flux_target = a2o_target[0]
    flux_count = a2o_count[0]
    flux_weight = a2o_weight[0]
    warmth_receiver = water_air_receiver[0]
    warmth_live_tally = water_air_live_tally[0]
    warmth_overlay_share = water_air_overlay_share[0]
    flux_on_ocean = position_combination(
        received_energy_rate, flux_target, flux_count, flux_weight, ocean_dest
    ).reshape(water_anomaly.shape[1], water_anomaly.shape[2])
    water_warmth_on_air = position_combination(
        received_water_warmth,
        warmth_receiver,
        warmth_live_tally,
        warmth_overlay_share,
        atmosphere_destination_tile,
    ).reshape(atmos.shape[1], atmos.shape[2])
    current_condition = atmos
    for step in range(2):
        widened_array = with_halo(current_condition, (("tiles", 1),), 1)
        current_condition = air_advance_interval(
            widened_array, air_mixing_numbers, air_vertical_operator, water_warmth_on_air
        )
    future_energy_exchange = AIR_EXCHANGER * (water_warmth_on_air - current_condition[-1])
    ocean_wide = with_halo(water_anomaly, (("tiles", 1),), 1)
    ocean_next = ocean_advance(ocean_wide, ocean_kappa, ocean_column, water_entries, flux_on_ocean)
    return (current_condition, ocean_next, future_energy_exchange)


def solution(mesh):
    placed = (
        P("members", "tiles", None),
        P("members", "tiles", None),
        P("tiles", "members"),
        P("tiles", None),
        P("tiles", None),
        P("tiles", None),
        P(),
        P(),
        P("tiles", None, None),
        P("tiles", None, None),
        P("tiles", None),
        P("tiles", None, None, None),
        P("tiles", None, None),
        P("tiles", None, None),
        P("tiles", None),
        P("tiles", None, None, None),
    )
    return jax.shard_map(
        shards,
        mesh=mesh,
        in_specs=placed,
        out_specs=(P("members", "tiles", None), P("members", "tiles", None), P("tiles", "members")),
        check_vma=False,
    )
```

profile of v0, /device:TPU:1, one launch (start us, length us, event | category | flops | bytes accessed | tf_op | source)
XLA Modules:
  0.0 115.5 jit_solution(5094915058676689040)
XLA Ops:
  0.6 2.5 %fusion.51 = (f32[30,1,1152]{2,1,0:T(1,128)}, f32[30,1,1152]{2,1,0:T(1,128)}) fusion(f32[30,24,1152]{2,1,0:T(8,128)} %param.16), kind=kLoop, calls=%fused_computation.92 | loop fusion | bytes 552960 | tf_op jit(solution)/shard_map/slice | solution.py:17
  3.1 2.0 %collective-permute-start = (f32[30,1,1152]{2,1,0:T(1,128)}, f32[30,1,1152]{2,1,0:T(1,128)}, u32[]{:S(2)}, u32[]{:S(2)}) collective-permute-start(f32[30,1,1152]{2,1,0:T(1,128)} %get-tuple-element.16), channel_id=1, source_target_pairs={{1,0},{2,1},{3,2},{4,3},{5,4},{6,5},{7,6},{8,7},{9,8},{10,9},{11,1... | collective-permute-start | bytes 414728 | tf_op jit(solution)/shard_map/ppermute | solution.py:23
  5.1 4.5 %collective-permute-start.1 = (f32[30,1,1152]{2,1,0:T(1,128)}, f32[30,1,1152]{2,1,0:T(1,128)}, u32[]{:S(2)}, u32[]{:S(2)}) collective-permute-start(f32[30,1,1152]{2,1,0:T(1,128)} %get-tuple-element.17), channel_id=1, source_target_pairs={{0,1},{1,2},{2,3},{3,4},{4,5},{5,6},{6,7},{7,8},{8,9},{9,10},{10,1... | collective-permute-start | bytes 414728 | tf_op jit(solution)/shard_map/ppermute | solution.py:21
  9.6 0.7 compare_select_fusion
  10.4 0.9 reshape.135
  11.3 2.3 %gather_fusion.1 = f32[768,128]{1,0:T(8,128)} fusion(f32[216,128]{1,0:T(8,128)S(1)} %reshape.135, s32[1024]{0:T(1024)S(1)} %pad_clamp_fusion), kind=kCustom, calls=%fused_computation.1 | custom fusion | bytes 789504 | tf_op jit(solution)/shard_map/gather | solution.py:105
  13.6 5.9 %all-to-all-start.1 = ((f32[16,48,128]{2,1,0:T(8,128)}), f32[16,48,128]{2,1,0:T(8,128)}, u32[]{:S(2)}, u32[]{:S(2)}) async-start(f32[16,48,128]{2,1,0:T(8,128)} %bitcast.14), calls=%async_computation.1 | async-start | bytes 786432 | tf_op jit(solution)/shard_map/all_to_all | solution.py:108
  19.4 3.3 %copy.35 = f32[50,8,1440]{2,0,1:T(8,128)S(1)} copy(f32[50,8,1440]{2,1,0:T(8,128)} %param.17) | data formatting | bytes 4608000 | tf_op args[1]
  22.7 1.0 fusion.54
  23.7 2.0 %collective-permute-start.4 = (f32[50,1,1440]{2,0,1:T(8,128)}, f32[50,1,1440]{2,0,1:T(8,128)}, u32[]{:S(2)}, u32[]{:S(2)}) collective-permute-start(f32[50,1,1440]{2,0,1:T(8,128)} %get-tuple-element.22), channel_id=1, source_target_pairs={{1,0},{2,1},{3,2},{4,3},{5,4},{6,5},{7,6},{8,7},{9,8},{10,9},{11,1... | collective-permute-start | bytes 864008 | tf_op jit(solution)/shard_map/ppermute | solution.py:23
  25.8 3.5 %collective-permute-start.5 = (f32[50,1,1440]{2,0,1:T(8,128)}, f32[50,1,1440]{2,0,1:T(8,128)}, u32[]{:S(2)}, u32[]{:S(2)}) collective-permute-start(f32[50,1,1440]{2,0,1:T(8,128)} %get-tuple-element.23), channel_id=1, source_target_pairs={{0,1},{1,2},{2,3},{3,4},{4,5},{5,6},{6,7},{7,8},{8,9},{9,10},{10,1... | collective-permute-start | bytes 864008 | tf_op jit(solution)/shard_map/ppermute | solution.py:21
  29.3 1.0 fusion.50
  30.3 0.9 fusion.53
  31.2 3.5 %fusion.52 = (f32[50,8,1439]{2,0,1:T(8,128)}, f32[50,8,1439]{2,0,1:T(8,128)}) fusion(f32[50,8,1440]{2,0,1:T(8,128)S(1)} %copy.35), kind=kLoop, calls=%fused_computation.93 | loop fusion | bytes 9209600 | tf_op jit(solution)/shard_map/jit(_roll_static)/slice | solution.py:67
  34.7 3.9 %fusion.49 = (f32[30,24,1151]{2,1,0:T(8,128)}, f32[30,24,1151]{2,1,0:T(8,128)}) fusion(f32[30,24,1152]{2,1,0:T(8,128)S(1)} %copy-done.2), kind=kLoop, calls=%fused_computation.90 | loop fusion | bytes 13259520 | tf_op jit(solution)/shard_map/jit(_roll_static)/slice | solution.py:47
  38.6 0.7 fusion.47
  39.4 0.6 pad_clamp_fusion.1
  40.1 5.7 %fusion.17 = f32[30,24,1152]{2,1,0:T(8,128)} fusion(f32[30,24,1152]{2,1,0:T(8,128)S(1)} %copy-done.2, f32[30,1,1152]{2,1,0:T(1,128)} %collective-permute-done.1, f32[30,1,1152]{2,1,0:T(1,128)} %collective-permute-done, f32[30,24,1151]{2,1,0:T(8,128)} %get-tuple-element.13, f32[30,24,1]{2,1,0:T(8,128)} %get-tuple-element.15, ...), kind=kLoop, calls=%fused_computation.32 | loop fusion | flops 9123840 | bytes 13658112 | tf_op jit(solution)/shard_map/add | solution.py:53
  45.8 1.1 copy-done.9
  47.0 5.7 %fusion.19 = f32[50,8,1440]{2,0,1:T(8,128)S(1)} fusion(f32[50,8,1440]{2,0,1:T(8,128)S(1)} %copy-done.4, f32[50,1,1440]{2,0,1:T(8,128)} %collective-permute-done.5, f32[50,1,1440]{2,0,1:T(8,128)} %collective-permute-done.4, f32[50,8,1439]{2,0,1:T(8,128)S(1)} %copy-done.9, f32[50,8,1]{2,0,1:T(8,128)S(1)} %copy-done.16, f32[50,8,1]{2,0,1:T(8,128)S(1)} %copy-done.15, ...), kind=kOutput, calls=%fused_computation.37 | convolution fusion | flops 353088000 | bytes 9894160 | tf_op jit(solution)/shard_map/kl,lyx->kyx/dot_general | solution.py:69
  52.7 1.5 %copy-done.6 = f32[50,8,1440]{2,0,1:T(8,128)} copy-done((f32[50,8,1440]{2,0,1:T(8,128)}, f32[50,8,1440]{2,0,1:T(8,128)S(1)}, u32[]{:S(2)}) %copy-start.6) | copy-done | bytes 2304024
  54.3 1.8 %convolution_bitcast_fusion.1 = f32[90,128]{1,0:T(8,128)S(1)} fusion(f32[16,48,128]{2,1,0:T(8,128)} %all-to-all-done.1, f32[1,16,48,128]{3,2,1,0:T(8,128)} %param.27, f32[16,48]{1,0:T(8,128)S(1)} %fusion.48, s32[16,48]{1,0:T(8,128)S(1)} %bitcast.69), kind=kOutput, calls=%fused_computation.51 | convolution fusion | flops 106434048 | bytes 838656 | tf_op jit(solution)/shard_map/scj,scb->jb/dot_general | solution.py:36
  56.2 1.4 %fusion.43 = (f32[8,1440]{1,0:T(8,128)S(1)}, f32[8,1440]{1,0:T(8,128)}) fusion(f32[1,8,1440]{2,0,1:T(1,128)S(1)} %slice.168, f32[8,1440]{1,0:T(8,128)S(1)} %reshape.136, s32[8,1440]{1,0:T(8,128)S(1)} %copy-done.17, f32[50,8,1440]{2,1,0:T(8,128)} %param.17), kind=kLoop, calls=%fused_computation.77 | loop fusion | flops 57600 | bytes 276480 | tf_op jit(solution)/shard_map/add | solution.py:75
  57.6 0.9 reshape.133
  58.5 2.3 %gather_fusion = f32[768,128]{1,0:T(8,128)} fusion(f32[90,128]{1,0:T(8,128)S(1)} %reshape.133, s32[1024]{0:T(1024)S(1)} %copy-done.19), kind=kCustom, calls=%fused_computation | custom fusion | bytes 789504 | tf_op jit(solution)/shard_map/gather | solution.py:106
  60.8 5.8 %all-to-all-start = ((f32[16,48,128]{2,1,0:T(8,128)}), f32[16,48,128]{2,1,0:T(8,128)}, u32[]{:S(2)}, u32[]{:S(2)}) async-start(f32[16,48,128]{2,1,0:T(8,128)} %bitcast.67), calls=%async_computation | async-start | bytes 786432 | tf_op jit(solution)/shard_map/all_to_all | solution.py:109
  66.6 5.9 %convolution_add_fusion = f32[30,24,1152]{2,0,1:T(8,128)S(1)} fusion(f32[30,24,1152]{2,1,0:T(8,128)} %fusion.17, f32[30,24,1152]{2,1,0:T(8,128)S(1)} %copy-done.2, f32[30,30]{1,0:T(8,128)S(1)} %copy-done.18), kind=kOutput, calls=%fused_computation.9 | convolution fusion | flops 299427840 | bytes 9956880 | tf_op jit(solution)/shard_map/kl,lyx->kyx/dot_general | solution.py:49
  72.5 0.7 slice.147
  73.3 1.9 %copy.39 = f32[29,24,1152]{2,1,0:T(8,128)S(1)} copy(f32[29,24,1152]{2,0,1:T(8,128)S(1)} %bitcast.66) | data formatting | bytes 6414336
  75.1 0.4 slice.169
  75.5 0.4 pad_maximum_fusion.10
  76.0 2.9 %copy.37 = f32[50,8,1440]{2,1,0:T(8,128)} copy(f32[50,8,1440]{2,0,1:T(8,128)S(1)} %pad_maximum_fusion.10) | data formatting | bytes 4608000
  78.8 2.1 %convolution_bitcast_fusion = f32[216,128]{1,0:T(8,128)S(1)} fusion(f32[16,48,128]{2,1,0:T(8,128)} %all-to-all-done, f32[1,16,48,128]{3,2,1,0:T(8,128)} %param.31, s32[16,48]{1,0:T(8,128)S(1)} %bitcast.68, f32[16,48]{1,0:T(8,128)S(1)} %copy-done.20), kind=kOutput, calls=%fused_computation.50 | convolution fusion | flops 255166464 | bytes 903168 | tf_op jit(solution)/shard_map/scj,scb->jb/dot_general | solution.py:36
  81.0 0.7 copy-done.10
  81.7 1.0 multiply_add_fusion.1
  82.6 0.9 fusion.35
  83.6 0.2 pad_maximum_fusion
  83.8 3.9 %fusion.4 = (f32[30,24,1151]{2,1,0:T(8,128)}, f32[30,24,1151]{2,1,0:T(8,128)}) fusion(f32[1,24,1152]{2,1,0:T(8,128)S(1)} %multiply_add_fusion.1, f32[29,24,1152]{2,1,0:T(8,128)S(1)} %copy.39), kind=kLoop, calls=%fused_computation.14 | loop fusion | flops 1657440 | bytes 9947520 | tf_op jit(solution)/shard_map/concatenate | solution.py:58
  87.7 2.1 %collective-permute-start.2 = (f32[30,1,1152]{2,1,0:T(1,128)}, f32[30,1,1152]{2,1,0:T(1,128)}, u32[]{:S(2)}, u32[]{:S(2)}) collective-permute-start(f32[30,1,1152]{2,1,0:T(1,128)} %get-tuple-element.10), channel_id=1, source_target_pairs={{1,0},{2,1},{3,2},{4,3},{5,4},{6,5},{7,6},{8,7},{9,8},{10,9},{11,1... | collective-permute-start | bytes 414728 | tf_op jit(solution)/shard_map/ppermute | solution.py:23
  89.8 3.7 %collective-permute-start.3 = (f32[30,1,1152]{2,1,0:T(1,128)}, f32[30,1,1152]{2,1,0:T(1,128)}, u32[]{:S(2)}, u32[]{:S(2)}) collective-permute-start(f32[30,1,1152]{2,1,0:T(1,128)} %get-tuple-element.11), channel_id=1, source_target_pairs={{0,1},{1,2},{2,3},{3,4},{4,5},{5,6},{6,7},{7,8},{8,9},{9,10},{10,1... | collective-permute-start | bytes 414728 | tf_op jit(solution)/shard_map/ppermute | solution.py:21
  93.5 5.3 %fusion = f32[24,1152,30]{1,2,0:T(8,128)} fusion(f32[30,24,1152]{2,1,0:T(8,128)S(1)} %pad_maximum_fusion, f32[30,30]{1,0:T(8,128)S(1)} %copy-done.18), kind=kOutput, calls=%fused_computation.10 | convolution fusion | flops 298598400 | bytes 6639120 | tf_op jit(solution)/shard_map/kl,lyx->kyx/dot_general | solution.py:49
  98.8 1.6 %reshape.137 = f32[24,1152]{1,0:T(8,128)} reshape(f32[216,128]{1,0:T(8,128)} %copy-done.10) | data formatting | bytes 221184 | tf_op jit(solution)/shard_map/reshape | solution.py:126
  100.6 1.8 %copy-done.5 = f32[24,1152,30]{1,2,0:T(8,128)S(1)} copy-done((f32[24,1152,30]{1,2,0:T(8,128)S(1)}, f32[24,1152,30]{1,2,0:T(8,128)}, u32[]{:S(2)}) %copy-start.5) | copy-done | bytes 3317784
  102.4 8.6 %fusion.11 = f32[30,24,1152]{2,1,0:T(8,128)S(1)} fusion(f32[30,1,1152]{2,1,0:T(1,128)} %collective-permute-done.3, f32[1,24,1152]{2,1,0:T(8,128)S(1)} %multiply_add_fusion.1, f32[29,24,1152]{2,1,0:T(8,128)S(1)} %copy.39, f32[30,1,1152]{2,1,0:T(1,128)} %collective-permute-done.2, f32[30,24,1151]{2,1,0:T(8,128)} %get-tuple-element.7, ...), kind=kLoop, calls=%fused_computation.22 | loop fusion | flops 12441600 | bytes 16975872 | tf_op jit(solution)/shard_map/add | solution.py:53
  111.1 0.2 slice.160
  111.3 0.6 copy-done.11
  112.0 1.6 %fusion.41 = f32[24,1152]{1,0:T(8,128)} fusion(f32[24,1152]{1,0:T(8,128)S(1)} %copy-done.14, f32[30,24,1152]{2,1,0:T(8,128)S(1)} %fusion.11, f32[1,24,1152]{2,0,1:T(1,128)S(1)} %copy-done.11, f32[30,24,1152]{2,1,0:T(8,128)} %param.16), kind=kLoop, calls=%fused_computation.71 | loop fusion | flops 221184 | bytes 552960 | tf_op jit(solution)/shard_map/mul | solution.py:133
  113.5 1.9 %pad_maximum_fusion.7 = f32[30,24,1152]{2,1,0:T(8,128)} fusion(f32[1,24,1152]{2,1,0:T(8,128)S(1)} %multiply_add_fusion, f32[29,24,1152]{2,1,0:T(8,128)S(1)} %slice.160), kind=kLoop, calls=%fused_computation.34 | loop fusion | flops 829440 | bytes 6635520 | tf_op jit(solution)/shard_map/concatenate | solution.py:58
  (69 shorter events, 0.8 us)
Async XLA Ops:
  0.6 45.1 %copy-start = (f32[50,50]{1,0:T(8,128)S(1)}, f32[50,50]{1,0:T(8,128)}, u32[]{:S(2)}) copy-start(f32[50,50]{1,0:T(8,128)} %param.23) | copy-start | bytes 30004
  3.1 36.8 %collective-permute-start = (f32[30,1,1152]{2,1,0:T(1,128)}, f32[30,1,1152]{2,1,0:T(1,128)}, u32[]{:S(2)}, u32[]{:S(2)}) collective-permute-start(f32[30,1,1152]{2,1,0:T(1,128)} %get-tuple-element.16), channel_id=1, source_target_pairs={{1,0},{2,1},{3,2},{4,3},{5,4},{6,5},{7,6},{8,7},{9,8},{10,9},{11,1... | collective-permute-start | bytes 414728 | tf_op jit(solution)/shard_map/ppermute | solution.py:23
  5.1 34.9 %collective-permute-start.1 = (f32[30,1,1152]{2,1,0:T(1,128)}, f32[30,1,1152]{2,1,0:T(1,128)}, u32[]{:S(2)}, u32[]{:S(2)}) collective-permute-start(f32[30,1,1152]{2,1,0:T(1,128)} %get-tuple-element.17), channel_id=1, source_target_pairs={{0,1},{1,2},{2,3},{3,4},{4,5},{5,6},{6,7},{7,8},{8,9},{9,10},{10,1... | collective-permute-start | bytes 414728 | tf_op jit(solution)/shard_map/ppermute | solution.py:21
  13.6 40.7 %all-to-all-start.1 = ((f32[16,48,128]{2,1,0:T(8,128)}), f32[16,48,128]{2,1,0:T(8,128)}, u32[]{:S(2)}, u32[]{:S(2)}) async-start(f32[16,48,128]{2,1,0:T(8,128)} %bitcast.14), calls=%async_computation.1 | async-start | bytes 786432 | tf_op jit(solution)/shard_map/all_to_all | solution.py:108
  19.4 9.9 %copy-start.2 = (f32[30,24,1152]{2,1,0:T(8,128)S(1)}, f32[30,24,1152]{2,1,0:T(8,128)}, u32[]{:S(2)}) copy-start(f32[30,24,1152]{2,1,0:T(8,128)} %param.16) | copy-start | bytes 9953284
  22.7 8.4 %copy-start.3 = (f32[50,8,1440]{2,0,1:T(8,128)}, f32[50,8,1440]{2,0,1:T(8,128)S(1)}, u32[]{:S(2)}) copy-start(f32[50,8,1440]{2,0,1:T(8,128)S(1)} %copy.35) | copy-start | bytes 6912004
  23.7 22.0 %collective-permute-start.4 = (f32[50,1,1440]{2,0,1:T(8,128)}, f32[50,1,1440]{2,0,1:T(8,128)}, u32[]{:S(2)}, u32[]{:S(2)}) collective-permute-start(f32[50,1,1440]{2,0,1:T(8,128)} %get-tuple-element.22), channel_id=1, source_target_pairs={{1,0},{2,1},{3,2},{4,3},{5,4},{6,5},{7,6},{8,7},{9,8},{10,9},{11,1... | collective-permute-start | bytes 864008 | tf_op jit(solution)/shard_map/ppermute | solution.py:23
  25.8 20.0 %collective-permute-start.5 = (f32[50,1,1440]{2,0,1:T(8,128)}, f32[50,1,1440]{2,0,1:T(8,128)}, u32[]{:S(2)}, u32[]{:S(2)}) collective-permute-start(f32[50,1,1440]{2,0,1:T(8,128)} %get-tuple-element.23), channel_id=1, source_target_pairs={{0,1},{1,2},{2,3},{3,4},{4,5},{5,6},{6,7},{7,8},{8,9},{9,10},{10,1... | collective-permute-start | bytes 864008 | tf_op jit(solution)/shard_map/ppermute | solution.py:21
  34.6 3.9 %copy-start.24 = (s32[1,16]{1,0:T(1,128)S(1)}, s32[1,16]{1,0:T(1,128)}, u32[]{:S(2)}) copy-start(s32[1,16]{1,0:T(1,128)} %param.26) | copy-start | bytes 196
  34.7 4.0 %copy-start.22 = (s32[1,16,48]{2,1,0:T(8,128)S(1)}, s32[1,16,48]{2,1,0:T(8,128)}, u32[]{:S(2)}) copy-start(s32[1,16,48]{2,1,0:T(8,128)} %param.28) | copy-start | bytes 9220
  34.7 4.0 %copy-start.25 = (s32[1,16]{1,0:T(1,128)S(1)}, s32[1,16]{1,0:T(1,128)}, u32[]{:S(2)}) copy-start(s32[1,16]{1,0:T(1,128)} %param.30) | copy-start | bytes 196
  34.7 4.7 %copy-start.17 = (s32[8,1440]{1,0:T(8,128)S(1)}, s32[8,1440]{1,0:T(8,128)}, u32[]{:S(2)}) copy-start(s32[8,1440]{1,0:T(8,128)} %param.19) | copy-start | bytes 138244
  34.7 5.3 %copy-start.12 = (f32[24,1152]{1,0:T(8,128)S(1)}, f32[24,1152]{1,0:T(8,128)}, u32[]{:S(2)}) copy-start(f32[24,1152]{1,0:T(8,128)} %param.20) | copy-start | bytes 331780
  40.0 5.8 %copy-start.4 = (f32[50,8,1440]{2,0,1:T(8,128)S(1)}, f32[50,8,1440]{2,0,1:T(8,128)}, u32[]{:S(2)}) copy-start(f32[50,8,1440]{2,0,1:T(8,128)} %copy-done.3) | copy-start | bytes 6912004
  40.0 5.8 %copy-start.8 = (f32[50,8,1439]{2,0,1:T(8,128)S(1)}, f32[50,8,1439]{2,0,1:T(8,128)}, u32[]{:S(2)}) copy-start(f32[50,8,1439]{2,0,1:T(8,128)} %get-tuple-element.18) | copy-start | bytes 6907204
  40.0 6.9 %copy-start.9 = (f32[50,8,1439]{2,0,1:T(8,128)S(1)}, f32[50,8,1439]{2,0,1:T(8,128)}, u32[]{:S(2)}) copy-start(f32[50,8,1439]{2,0,1:T(8,128)} %get-tuple-element.19) | copy-start | bytes 6907204
  40.0 6.9 %copy-start.15 = (f32[50,8,1]{2,0,1:T(8,128)S(1)}, f32[50,8,1]{2,0,1:T(8,128)}, u32[]{:S(2)}) copy-start(f32[50,8,1]{2,0,1:T(8,128)} %get-tuple-element.20) | copy-start | bytes 4804
  40.0 6.9 %copy-start.16 = (f32[50,8,1]{2,0,1:T(8,128)S(1)}, f32[50,8,1]{2,0,1:T(8,128)}, u32[]{:S(2)}) copy-start(f32[50,8,1]{2,0,1:T(8,128)} %get-tuple-element.21) | copy-start | bytes 4804
  40.0 6.9 %copy-start.26 = (f32[8,1440]{1,0:T(8,128)S(1)}, f32[8,1440]{1,0:T(8,128)}, u32[]{:S(2)}) copy-start(f32[8,1440]{1,0:T(8,128)} %param.21) | copy-start | bytes 138244
  46.9 7.3 %copy-start.23 = (s32[1,16,48]{2,1,0:T(8,128)S(1)}, s32[1,16,48]{2,1,0:T(8,128)}, u32[]{:S(2)}) copy-start(s32[1,16,48]{2,1,0:T(8,128)} %param.25) | copy-start | bytes 9220
  46.9 11.6 %copy-start.19 = (s32[1024]{0:T(1024)S(1)}, s32[1024]{0:T(1024)}, u32[]{:S(2)}) copy-start(s32[1024]{0:T(1024)} %pad_clamp_fusion.1) | copy-start | bytes 12292
  52.7 1.5 %copy-start.6 = (f32[50,8,1440]{2,0,1:T(8,128)}, f32[50,8,1440]{2,0,1:T(8,128)S(1)}, u32[]{:S(2)}) copy-start(f32[50,8,1440]{2,0,1:T(8,128)S(1)} %fusion.19) | copy-start | bytes 6912004
  54.2 12.4 %copy-start.18 = (f32[30,30]{1,0:T(8,128)S(1)}, f32[30,30]{1,0:T(8,128)}, u32[]{:S(2)}) copy-start(f32[30,30]{1,0:T(8,128)} %param.22) | copy-start | bytes 10804
  60.8 18.0 %all-to-all-start = ((f32[16,48,128]{2,1,0:T(8,128)}), f32[16,48,128]{2,1,0:T(8,128)}, u32[]{:S(2)}, u32[]{:S(2)}) async-start(f32[16,48,128]{2,1,0:T(8,128)} %bitcast.67), calls=%async_computation | async-start | bytes 786432 | tf_op jit(solution)/shard_map/all_to_all | solution.py:109
  73.3 1.9 %copy-start.7 = (f32[50,8,1440]{2,0,1:T(8,128)S(1)}, f32[50,8,1440]{2,0,1:T(8,128)}, u32[]{:S(2)}) copy-start(f32[50,8,1440]{2,0,1:T(8,128)} %copy-done.6) | copy-start | bytes 6912004
  75.9 2.9 %copy-start.20 = (f32[16,48]{1,0:T(8,128)S(1)}, f32[16,48]{1,0:T(8,128)}, u32[]{:S(2)}) copy-start(f32[16,48]{1,0:T(8,128)} %fusion.47) | copy-start | bytes 9220
  75.9 2.9 %copy-start.21 = (s32[1,16,48]{2,1,0:T(8,128)S(1)}, s32[1,16,48]{2,1,0:T(8,128)}, u32[]{:S(2)}) copy-start(s32[1,16,48]{2,1,0:T(8,128)} %param.29) | copy-start | bytes 9220
  81.0 0.7 copy-start.10
  87.7 12.9 %collective-permute-start.2 = (f32[30,1,1152]{2,1,0:T(1,128)}, f32[30,1,1152]{2,1,0:T(1,128)}, u32[]{:S(2)}, u32[]{:S(2)}) collective-permute-start(f32[30,1,1152]{2,1,0:T(1,128)} %get-tuple-element.10), channel_id=1, source_target_pairs={{1,0},{2,1},{3,2},{4,3},{5,4},{6,5},{7,6},{8,7},{9,8},{10,9},{11,1... | collective-permute-start | bytes 414728 | tf_op jit(solution)/shard_map/ppermute | solution.py:23
  89.8 10.8 %collective-permute-start.3 = (f32[30,1,1152]{2,1,0:T(1,128)}, f32[30,1,1152]{2,1,0:T(1,128)}, u32[]{:S(2)}, u32[]{:S(2)}) collective-permute-start(f32[30,1,1152]{2,1,0:T(1,128)} %get-tuple-element.11), channel_id=1, source_target_pairs={{0,1},{1,2},{2,3},{3,4},{4,5},{5,6},{6,7},{7,8},{8,9},{9,10},{10,1... | collective-permute-start | bytes 414728 | tf_op jit(solution)/shard_map/ppermute | solution.py:21
  100.4 2.0 %copy-start.5 = (f32[24,1152,30]{1,2,0:T(8,128)S(1)}, f32[24,1152,30]{1,2,0:T(8,128)}, u32[]{:S(2)}) copy-start(f32[24,1152,30]{1,2,0:T(8,128)} %fusion) | copy-start | bytes 9953284
  100.4 2.0 %copy-start.13 = (f32[24,1152]{1,0:T(8,128)S(1)}, f32[24,1152]{1,0:T(8,128)}, u32[]{:S(2)}) copy-start(f32[24,1152]{1,0:T(8,128)} %param.20) | copy-start | bytes 331780
  111.0 0.9 copy-start.11
  111.0 0.9 copy-start.14
  112.0 3.5 %copy-start.1 = (f32[50,50]{1,0:T(8,128)S(1)}, f32[50,50]{1,0:T(8,128)}, u32[]{:S(2)}) copy-start(f32[50,50]{1,0:T(8,128)} %param.23) | copy-start | bytes 30004
where the time goes:
time: 117 us; the launch traced here: 115 us
  local copies, waits for them, and re-layouts  36.2 us (31%)
  starting transfers between devices  29.4 us (25%)
  other arithmetic  27.9 us (24%)
  matrix products  20.9 us (18%)
    add x2, other arithmetic, air_advance_interval(): interior_points + mixing_coefficient * (beside - 4.0 * interior_points)  14.3 us
    unnamed x57, local copies, waits for them, and re-layouts  13.9 us
    ppermute x3, starting transfers between devices, with_halo(): lax.ppermute(tail, axis, [(i, (i + 1) % count) for i in range(ends)])  11.7 us
    dot_general x2, matrix products, air_advance_interval(): jnp.einsum('kl,lyx->kyx', vertical_linear_system, interior_points, precis...  11.2 us
    concatenate x5, other arithmetic, air_advance_interval(): return jnp.concatenate([advanced_condition[:-1], bottom_layer[None]], 0)  7.13 us
    ppermute x3, starting transfers between devices, with_halo(): lax.ppermute(head, axis, [((i + 1) % count, i) for i in range(ends)])  6.06 us
    all_to_all x1, starting transfers between devices, shards(): lax.all_to_all(flux_send, 'tiles', split_axis=0, concat_axis=0, tiled=True)  5.85 us
    all_to_all x1, starting transfers between devices, shards(): lax.all_to_all(sent_water_warmth, 'tiles', split_axis=0, concat_axis=0, t...  5.76 us
  transfers between devices with their start and end apart: 8, of which 0 were waited for; matrix products, arithmetic and copies ran while one was open for 43% of the time, Pallas kernels for 0%

commit v1 on v0

v1 whole, which is shorter than its diff:
```python
import functools

import jax
import jax.numpy as jnp
from jax import lax
from jax.experimental import pallas as pl
from jax.experimental.pallas import tpu as pltpu
from jax.sharding import PartitionSpec as P

LANES = 128
ENTRIES = 2
AIR_EXCHANGER = 0.3
COUPLE_OCEAN = 0.5
VMEM_BYTES = 52 * 1024 * 1024


def round_up(value, unit):
    return -(-value // unit) * unit


def offsets_of(tiles, count):
    leading = [0, tiles - 1, tiles // 2]
    return (leading + [v for v in range(tiles) if v not in leading])[:count]


def split_product(matrix, cells):
    high = cells.astype(jnp.bfloat16).astype(jnp.float32)
    low = cells - high
    stacked = jnp.concatenate([high, low, high], axis=0).astype(jnp.bfloat16)
    return jnp.dot(matrix, stacked, preferred_element_type=jnp.float32)


def lane_iota(shape):
    return lax.broadcasted_iota(jnp.int32, shape, len(shape) - 1)


def exchange_kernel(
    dims,
    atmos, water, flux, mask, kap_a, kap_o, mat_a, mat_o,
    f_src, f_tgt, f_cnt, f_wgt, w_src, w_tgt, w_cnt, w_wgt,
    u2_out, o2_out, g_out, d_out, fl_out,
    in_a, u, u1, u2, in_o, o, o2, surf,
    f_blocks, w_blocks, f_send, w_send, f_recv, w_recv, f_wbuf, w_wbuf,
    eff, f_terms, w_terms, r_a, r_o, t_o, r_halo, g_rows, lanes_o, kap_rows,
    dma, f_ss, f_rs, w_ss, w_rs, h_ss, h_rs,
):
    n, la, ya, xa, lo, yo, xo, cap, nf, nw = dims
    lap, lop = round_up(la + 1, 8), round_up(lo, 8)
    xop = round_up(xo, LANES)
    tail = xo % LANES
    ja, jo = xa // LANES, xop // LANES
    me = lax.axis_index("tiles")
    offs = offsets_of(n, nw)

    def source_of(q):
        return lax.rem(me + offs[q], n)

    def dest_of(q):
        return lax.rem(me + (n - offs[q]), n)

    barrier = pltpu.get_barrier_semaphore()
    for q in range(1, nw):
        pl.semaphore_signal(barrier, inc=1, device_id={"tiles": source_of(q)})

    surf_copy = pltpu.make_async_copy(water.at[0], surf, dma.at[0])
    surf_copy.start()
    groups = ya // 8
    air_copies = [
        pltpu.make_async_copy(atmos.at[:, pl.ds(8 * i, 8), :], in_a.at[i], dma.at[1 + i])
        for i in range(groups)
    ]
    order = [0, groups - 1] + list(range(1, groups - 1))
    for i in order:
        air_copies[i].start()
    at = 1 + groups
    water_copy = pltpu.make_async_copy(water, in_o, dma.at[at])
    water_copy.start()
    at += 1
    wgt_copies = []
    for q in range(nw):
        wgt_copies.append(pltpu.make_async_copy(w_wgt.at[0, source_of(q)], w_wbuf.at[q], dma.at[at]))
        at += 1
    for q in range(nf):
        wgt_copies.append(pltpu.make_async_copy(f_wgt.at[0, source_of(q)], f_wbuf.at[q], dma.at[at]))
        at += 1
    for c in wgt_copies:
        c.start()

    for j in range(ja):
        f_blocks[pl.ds(j, ya, stride=ja), :] = flux[:, j * LANES : (j + 1) * LANES]
    surf_copy.wait()
    sea2 = mask[...].astype(jnp.float32)
    lanes_o[...] = jnp.zeros_like(lanes_o)
    lanes_o[:, 0:xo] = surf[...] * sea2
    w_blocks[...] = jnp.zeros_like(w_blocks)
    for j in range(jo):
        t_o[pl.ds(j, yo, stride=jo), :] = lanes_o[:, j * LANES : (j + 1) * LANES]
    for y in range(yo):
        first, shift = (y * xo) // LANES, (y * xo) % LANES
        tiles = t_o[y * jo : (y + 1) * jo, :]
        if shift == 0:
            w_blocks[first : first + jo, :] = tiles
        else:
            rolled = pltpu.roll(tiles, shift, 1)
            before = jnp.concatenate([w_blocks[first : first + 1, :], rolled[: jo - 1]], axis=0)
            w_blocks[first : first + jo, :] = jnp.where(
                lane_iota((jo, LANES)) < shift, before, rolled
            )

    def gather(dst, blocks, source, d):
        def body(i, carry):
            for k in range(8):
                c = i * 8 + k
                dst[pl.ds(c, 1), :] = blocks[pl.ds(source[0, d, c], 1), :]
            return carry

        lax.fori_loop(0, cap // 8, body, 0)

    for q in range(nw):
        gather(w_recv.at[0] if q == 0 else w_send.at[q - 1], w_blocks, w_src, dest_of(q))
    for q in range(nf):
        gather(f_recv.at[0] if q == 0 else f_send.at[q - 1], f_blocks, f_src, dest_of(q))

    pl.semaphore_wait(barrier, nw - 1)
    w_copies, f_copies = {}, {}
    for q in range(1, nw):
        w_copies[q] = pltpu.make_async_remote_copy(
            src_ref=w_send.at[q - 1], dst_ref=w_recv.at[q],
            send_sem=w_ss.at[q - 1], recv_sem=w_rs.at[q - 1], device_id={"tiles": dest_of(q)},
        )
    for q in range(1, nf):
        f_copies[q] = pltpu.make_async_remote_copy(
            src_ref=f_send.at[q - 1], dst_ref=f_recv.at[q],
            send_sem=f_ss.at[q - 1], recv_sem=f_rs.at[q - 1], device_id={"tiles": dest_of(q)},
        )
    for q in [2] + list(range(nw - 1, 2, -1)) + [1]:
        w_copies[q].start()
        if q in f_copies:
            f_copies[q].start()

    kap_rows[...] = jnp.zeros_like(kap_rows)

    def turn_air(i):
        air_copies[i].wait()
        for j in range(ja):
            cut = pl.ds(j * LANES, LANES)
            u[pl.ds(2 + 8 * i, 8), 0:la, cut] = jnp.swapaxes(in_a[i, :, :, cut], 0, 1)
        for r in range(8):
            u[2 + 8 * i + r, la : la + 1, :] = kap_a[8 * i + r : 8 * i + r + 1, :]
            if lap > la + 1:
                u[2 + 8 * i + r, la + 1 : lap, :] = jnp.zeros((lap - la - 1, xa), jnp.float32)

    up, down = lax.rem(me + 1, n), lax.rem(me + n - 1, n)

    def to_next(k, src, dst):
        return pltpu.make_async_remote_copy(
            src_ref=src, dst_ref=dst, send_sem=h_ss.at[k], recv_sem=h_rs.at[k],
            device_id={"tiles": up},
        )

    def to_prev(k, src, dst):
        return pltpu.make_async_remote_copy(
            src_ref=src, dst_ref=dst, send_sem=h_ss.at[k], recv_sem=h_rs.at[k],
            device_id={"tiles": down},
        )

    has_next, has_prev = me < n - 1, me > 0
    air_up = to_next(0, u.at[pl.ds(ya, 2)], u.at[pl.ds(0, 2)])
    air_down = to_prev(1, u.at[pl.ds(2, 2)], u.at[pl.ds(ya + 2, 2)])
    sea_up = to_next(2, o.at[yo], o.at[0])
    sea_down = to_prev(3, o.at[1], o.at[yo + 1])
    blk_up = to_next(4, r_a.at[pl.ds(ya * ja - 16, 16)], r_halo.at[0])
    blk_down = to_prev(5, r_a.at[pl.ds(0, 16)], r_halo.at[1])

    turn_air(0)

    @pl.when(has_prev)
    def _():
        air_down.start()

    turn_air(groups - 1)

    @pl.when(has_next)
    def _():
        air_up.start()

    water_copy.wait()
    for j in range(jo):
        width = min(LANES, xo - j * LANES)
        cut = pl.ds(j * LANES, width)
        o[pl.ds(1, yo), 0:lo, cut] = jnp.swapaxes(in_o[:, :, cut], 0, 1)
    for y in range(yo):
        o[1 + y, lo:lop, :] = jnp.zeros((lop - lo, xop), jnp.float32)
        head = o[1 + y, :, 0:LANES]
        last = o[1 + y, :, xop - LANES : xop]
        lane = lane_iota((lop, LANES))
        wrapped = jnp.where(
            lane == tail,
            pltpu.roll(head, tail, 1),
            jnp.where(lane == LANES - 1, pltpu.roll(last, LANES - tail, 1), 0.0),
        )
        o[1 + y, :, xop - LANES : xop] = jnp.where(lane < tail, last, wrapped)

    @pl.when(has_prev)
    def _():
        sea_down.start()

    @pl.when(has_next)
    def _():
        sea_up.start()

    for i in range(1, groups - 1):
        turn_air(i)

    def air_step(dst, dst_row, src, row):
        c = src[row]
        kap = u[dst_row[1], la : la + 1, :]
        beside = src[row - 1] + src[row + 1] + pltpu.roll(c, 1, 1) + pltpu.roll(c, xa - 1, 1)
        dst[dst_row[0]] = split_product(mat_a[...], c) + kap * (beside - 4.0 * c)

    def first_step(y):
        air_step(u1, (y + 1, y + 2), u, y + 2)

    lax.fori_loop(1, ya - 1, lambda y, c: (first_step(y), c)[1], 0)

    lanes_o[...] = jnp.zeros_like(lanes_o)
    lanes_o[:, 0:xo] = sea2
    kap_rows[:, 0:xo] = kap_o[...]

    def sea_step(y):
        c = o[y + 1]
        kap = kap_rows[pl.ds(y, 1), :]
        wet = lanes_o[pl.ds(y, 1), :]
        beside = o[y] + o[y + 2] + pltpu.roll(c, 1, 1) + pltpu.roll(c, xop - 1, 1)
        o2[y] = c + wet * (kap * (beside - 4.0 * c) + split_product(mat_o[...], c))

    lax.fori_loop(1, yo - 1, lambda y, c: (sea_step(y), c)[1], 0)

    @pl.when(has_prev)
    def _():
        air_up.wait_recv()

    @pl.when(jnp.logical_not(has_prev))
    def _():
        u[0:2] = jnp.zeros((2, lap, xa), jnp.float32)

    @pl.when(has_next)
    def _():
        air_down.wait_recv()

    @pl.when(jnp.logical_not(has_next))
    def _():
        u[ya + 2 : ya + 4] = jnp.zeros((2, lap, xa), jnp.float32)

    for y in (-1, 0, ya - 1, ya):
        first_step(y)

    u2_copies = []
    for i in range(groups):
        lax.fori_loop(
            8 * i,
            8 * i + 8,
            lambda y, c: (air_step(u2, (y, y + 2), u1, y + 1), c)[1],
            0,
        )
        copy = pltpu.make_async_copy(
            u2.at[pl.ds(8 * i, 8)], u2_out.at[pl.ds(8 * i, 8)], dma.at[1 + i]
        )
        copy.start()
        u2_copies.append(copy)

    @pl.when(has_prev)
    def _():
        sea_up.wait_recv()

    @pl.when(jnp.logical_not(has_prev))
    def _():
        o[0] = jnp.zeros((lop, xop), jnp.float32)

    @pl.when(has_next)
    def _():
        sea_down.wait_recv()

    @pl.when(jnp.logical_not(has_next))
    def _():
        o[yo + 1] = jnp.zeros((lop, xop), jnp.float32)

    sea_step(0)
    sea_step(yo - 1)
    o2_copy = pltpu.make_async_copy(o2, o2_out, dma.at[0])
    o2_copy.start()

    for c in wgt_copies:
        c.wait()
    for q in range(1, nw):
        w_copies[q].wait_recv()
    for q in range(1, nf):
        f_copies[q].wait_recv()

    def combine(count, recv, wbuf, terms, tgt, cnt, row, rows):
        for q in range(count):
            s = source_of(q)
            live = lane_iota((1, cap)) < cnt[0, s]
            eff[row : row + 1, cap * q : cap * (q + 1)] = jnp.where(live, tgt[0, pl.ds(s, 1), :], -1)
            value = wbuf[q] * recv[q]
            high = value.astype(jnp.bfloat16)
            terms[cap * q : cap * (q + 1), 0:LANES] = high
            terms[cap * q : cap * (q + 1), LANES:] = (value - high.astype(jnp.float32)).astype(jnp.bfloat16)
        slots = cap * count
        chosen = eff[row : row + 1, 0:slots] == lax.broadcasted_iota(jnp.int32, (rows, slots), 0)
        onehot = jnp.where(chosen, 1.0, 0.0).astype(jnp.bfloat16)
        both = jnp.dot(onehot, terms[...], preferred_element_type=jnp.float32)
        return both[:, :LANES] + both[:, LANES:]

    r_a[...] = combine(nw, w_recv, w_wbuf, w_terms, w_tgt, w_cnt, 0, r_a.shape[0]) * AIR_EXCHANGER

    @pl.when(has_next)
    def _():
        blk_up.start()

    @pl.when(has_prev)
    def _():
        blk_down.start()

    r_o[...] = combine(nf, f_recv, f_wbuf, f_terms, f_tgt, f_cnt, 1, r_o.shape[0]) * COUPLE_OCEAN
    for y in range(yo):
        first, shift = (y * xo) // LANES, (y * xo) % LANES
        here = r_o[first : first + jo, :]
        if shift:
            after = r_o[first + 1 : first + jo + 1, :]
            here = jnp.where(
                lane_iota((jo, LANES)) < LANES - shift,
                pltpu.roll(here, LANES - shift, 1),
                pltpu.roll(after, LANES - shift, 1),
            )
        t_o[y * jo : (y + 1) * jo, :] = here
    for j in range(jo):
        cut = slice(j * LANES, (j + 1) * LANES)
        fl_out[:, cut] = t_o[pl.ds(j, yo, stride=jo), :] * lanes_o[:, cut]

    for j in range(ja):
        g_rows[8 : 8 + ya, j * LANES : (j + 1) * LANES] = r_a[pl.ds(j, ya, stride=ja), :]
    g_rows[0:8, :] = jnp.zeros((8, xa), jnp.float32)
    g_rows[8 + ya : 16 + ya, :] = jnp.zeros((8, xa), jnp.float32)

    @pl.when(has_prev)
    def _():
        blk_up.wait_recv()
        for j in range(ja):
            g_rows[7:8, j * LANES : (j + 1) * LANES] = r_halo[0, 16 - ja + j : 17 - ja + j, :]

    @pl.when(has_next)
    def _():
        blk_down.wait_recv()
        for j in range(ja):
            g_rows[8 + ya : 9 + ya, j * LANES : (j + 1) * LANES] = r_halo[1, j : j + 1, :]

    g = g_rows[8 : 8 + ya, :]
    g_out[...] = g
    beside = (
        g_rows[7 : 7 + ya, :]
        + g_rows[9 : 9 + ya, :]
        + pltpu.roll(g, 1, 1)
        + pltpu.roll(g, xa - 1, 1)
    )
    d_out[...] = kap_a[...] * (beside - 4.0 * g) + g

    for c in u2_copies:
        c.wait()
    o2_copy.wait()
    for q in range(1, nw):
        w_copies[q].wait_send()
    for q in range(1, nf):
        f_copies[q].wait_send()

    @pl.when(has_next)
    def _():
        air_up.wait_send()
        sea_up.wait_send()
        blk_up.wait_send()

    @pl.when(has_prev)
    def _():
        air_down.wait_send()
        sea_down.wait_send()
        blk_down.wait_send()


def finish_kernel(la, lo, u2, g, d, column, o2, fl, air, sea, energy):
    turned = jnp.swapaxes(u2[...], 0, 1)
    warm = g[...]
    for k in range(la):
        level = turned[k] + column[k] * warm
        if k == la - 1:
            level = level + d[...]
            energy[...] = warm - AIR_EXCHANGER * level
        air[k] = level
    turned = jnp.swapaxes(o2[...], 0, 1)
    sea[0] = turned[0] + fl[...]
    for k in range(1, lo):
        sea[k] = turned[k]


def parts_of(matrix, rows):
    padded = jnp.pad(matrix, ((0, rows - matrix.shape[0]), (0, rows - matrix.shape[1])))
    high = lax.reduce_precision(padded, 8, 7)
    low = padded - high
    return jnp.concatenate([high, high, low], axis=1).astype(jnp.bfloat16)


def shards(
    tiles,
    atmos,
    water_anomaly,
    atm_flux,
    ocean_mask,
    air_mixing_numbers,
    ocean_kappa,
    air_vertical_operator,
    ocean_column,
    a2o_source,
    a2o_target,
    a2o_count,
    a2o_weight,
    water_air_provider,
    water_air_receiver,
    water_air_live_tally,
    water_air_overlay_share,
):
    la, ya, xa = atmos.shape
    lo, yo, xo = water_anomaly.shape
    cap = a2o_source.shape[2]
    air_blocks, sea_blocks = ya * xa // LANES, yo * xo // LANES
    nw = min(tiles, -(-ENTRIES * air_blocks // cap) + 1)
    nf = min(tiles, -(-ENTRIES * sea_blocks // cap) + 1)
    dims = (tiles, la, ya, xa, lo, yo, xo, cap, nf, nw)
    lap, lop = round_up(la + 1, 8), round_up(lo, 8)
    xop = round_up(xo, LANES)
    jo = xop // LANES

    level = jnp.arange(la)
    diagonal = jnp.where(level == la - 1, 1.0 - AIR_EXCHANGER, 1.0).astype(jnp.float32)
    step_matrix = air_vertical_operator + jnp.diag(diagonal)
    mat_a = parts_of(step_matrix, lap)
    mat_o = parts_of(ocean_column, lop)

    f32 = jnp.float32
    vm = pl.BlockSpec(memory_space=pltpu.VMEM)
    sm = pl.BlockSpec(memory_space=pltpu.SMEM)
    hb = pl.BlockSpec(memory_space=pl.ANY)
    S = jax.ShapeDtypeStruct
    u2, o2, g, d, fl = pl.pallas_call(
        functools.partial(exchange_kernel, dims),
        out_shape=(
            S((ya, lap, xa), f32),
            S((yo, lop, xop), f32),
            S((ya, xa), f32),
            S((ya, xa), f32),
            S((yo, xop), f32),
        ),
        in_specs=[hb, hb, vm, vm, vm, vm, vm, vm, sm, vm, sm, hb, sm, vm, sm, hb],
        out_specs=(hb, hb, vm, vm, vm),
        scratch_shapes=[
            pltpu.VMEM((ya // 8, la, 8, xa), f32),
            pltpu.VMEM((ya + 4, lap, xa), f32),
            pltpu.VMEM((ya + 2, lap, xa), f32),
            pltpu.VMEM((ya, lap, xa), f32),
            pltpu.VMEM((lo, yo, xo), f32),
            pltpu.VMEM((yo + 2, lop, xop), f32),
            pltpu.VMEM((yo, lop, xop), f32),
            pltpu.VMEM((yo, xo), f32),
            pltpu.VMEM((air_blocks, LANES), f32),
            pltpu.VMEM((round_up(sea_blocks + jo, 8), LANES), f32),
            pltpu.VMEM((nf - 1, cap, LANES), f32),
            pltpu.VMEM((nw - 1, cap, LANES), f32),
            pltpu.VMEM((nf, cap, LANES), f32),
            pltpu.VMEM((nw, cap, LANES), f32),
            pltpu.VMEM((nf, cap, LANES), f32),
            pltpu.VMEM((nw, cap, LANES), f32),
            pltpu.VMEM((8, round_up(cap * nw, LANES)), jnp.int32),
            pltpu.VMEM((nf * cap, 2 * LANES), jnp.bfloat16),
            pltpu.VMEM((nw * cap, 2 * LANES), jnp.bfloat16),
            pltpu.VMEM((air_blocks, LANES), f32),
            pltpu.VMEM((round_up(sea_blocks + 2, 8), LANES), f32),
            pltpu.VMEM((yo * jo, LANES), f32),
            pltpu.VMEM((2, 16, LANES), f32),
            pltpu.VMEM((ya + 16, xa), f32),
            pltpu.VMEM((yo, xop), f32),
            pltpu.VMEM((yo, xop), f32),
            pltpu.SemaphoreType.DMA((2 + ya // 8 + nw + nf,)),
            pltpu.SemaphoreType.DMA((nf - 1,)),
            pltpu.SemaphoreType.DMA((nf - 1,)),
            pltpu.SemaphoreType.DMA((nw - 1,)),
            pltpu.SemaphoreType.DMA((nw - 1,)),
            pltpu.SemaphoreType.DMA((6,)),
            pltpu.SemaphoreType.DMA((6,)),
        ],
        compiler_params=pltpu.CompilerParams(
            collective_id=0, has_side_effects=True, vmem_limit_bytes=VMEM_BYTES
        ),
    )(
        atmos, water_anomaly, atm_flux, ocean_mask, air_mixing_numbers, ocean_kappa, mat_a, mat_o,
        a2o_source, a2o_target, a2o_count, a2o_weight,
        water_air_provider, water_air_receiver, water_air_live_tally, water_air_overlay_share,
    )

    steps = ya // 8
    cut = round_up(-(-xop // steps), LANES)
    return pl.pallas_call(
        functools.partial(finish_kernel, la, lo),
        grid=(steps,),
        out_shape=(S((la, ya, xa), f32), S((lo, yo, xo), f32), S((ya, xa), f32)),
        in_specs=[
            pl.BlockSpec((8, lap, xa), lambda i: (i, 0, 0)),
            pl.BlockSpec((8, xa), lambda i: (i, 0)),
            pl.BlockSpec((8, xa), lambda i: (i, 0)),
            pl.BlockSpec(memory_space=pltpu.SMEM),
            pl.BlockSpec((yo, lop, cut), lambda i: (0, 0, i)),
            pl.BlockSpec((yo, cut), lambda i: (0, i)),
        ],
        out_specs=(
            pl.BlockSpec((la, 8, xa), lambda i: (0, i, 0)),
            pl.BlockSpec((lo, yo, cut), lambda i: (0, 0, i)),
            pl.BlockSpec((8, xa), lambda i: (i, 0)),
        ),
        compiler_params=pltpu.CompilerParams(vmem_limit_bytes=VMEM_BYTES),
    )(u2, g, d, step_matrix[:, la - 1], o2, fl)


def solution(mesh):
    placed = (
        P("members", "tiles", None),
        P("members", "tiles", None),
        P("tiles", "members"),
        P("tiles", None),
        P("tiles", None),
        P("tiles", None),
        P(),
        P(),
        P("tiles", None, None),
        P("tiles", None, None),
        P("tiles", None),
        P("tiles", None, None, None),
        P("tiles", None, None),
        P("tiles", None, None),
        P("tiles", None),
        P("tiles", None, None, None),
    )
    return jax.shard_map(
        functools.partial(shards, mesh.shape["tiles"]),
        mesh=mesh,
        in_specs=placed,
        out_specs=(P("members", "tiles", None), P("members", "tiles", None), P("tiles", "members")),
        check_vma=False,
    )
```

time: 117 us -> 49.7 us (0.42)
  Pallas kernels: 0 us -> 36.9 us
  starting transfers between devices: 29.4 us -> 0 us
  local copies, waits for them, and re-layouts: 36.2 us -> 9.65 us
  other arithmetic: 27.9 us -> 1.73 us
  matrix products: 20.9 us -> 0 us
    pallas_call x0 -> x2, Pallas kernels: none -> 36.9 us  [the longest x1 30.4 us: shards(): pl.pallas_call(functools.partial(exchange_kernel, dims), out_shape=(S((ya...]
    dot_general x5 -> x0, matrix products: 20.9 us -> none  [the longest x2 11.2 us: air_advance_interval(): jnp.einsum('kl,lyx->kyx', vertical_linear_system, interior_points, precis...]
    ppermute x6 -> x0, starting transfers between devices: 17.8 us -> none  [the longest x3 11.7 us: with_halo(): lax.ppermute(tail, axis, [(i, (i + 1) % count) for i in range(ends)])]
    add x5 -> x1, other arithmetic: 16.7 us -> 0.79 us  [shards(): step_matrix = air_vertical_operator + jnp.diag(diagonal)]
    slice x10 -> x1, local copies, waits for them, and re-layouts: 14 us -> 0.18 us  [shards(): step_matrix[:, la - 1]]
    all_to_all x2 -> x0, starting transfers between devices: 11.6 us -> none  [the longest x1 5.85 us: shards(): lax.all_to_all(flux_send, 'tiles', split_axis=0, concat_axis=0, tiled=True)]
    concatenate x6 -> x2, other arithmetic: 7.52 us -> 0.17 us  [parts_of(): return jnp.concatenate([high, high, low], axis=1).astype(jnp.bfloat16)]
    gather x2 -> x0, local copies, waits for them, and re-layouts: 4.56 us -> none  [the longest x1 2.28 us: shards(): flux_send = atmos_blocks[flux_list]]
  transfers between devices with their start and end apart: 8 -> 0, of which waited for: 0 -> 0; matrix products, arithmetic and copies ran while one was open for 43% -> 0% of each run, Pallas kernels for 0% -> 0%
where the time goes in v1:
time: 49.7 us; the launch traced here: 48.9 us
  Pallas kernels  36.9 us (74%)
  local copies, waits for them, and re-layouts  9.65 us (19%)
  other arithmetic  1.73 us (3%)
  between operations  0.68 us (1%)
    pallas_call x1, Pallas kernels, shards(): pl.pallas_call(functools.partial(exchange_kernel, dims), out_shape=(S((ya...  30.4 us
    unnamed x24, local copies, waits for them, and re-layouts  9.47 us
    pallas_call x1, Pallas kernels, shards(): pl.pallas_call(functools.partial(finish_kernel, la, lo), grid=(steps,), o...  6.51 us

profile of v1, /device:TPU:1, one launch (start us, length us, event | category | flops | bytes accessed | tf_op | source)
XLA Modules:
  0.0 48.9 jit_solution(11635180996524243237)
XLA Ops:
  0.6 0.8 %select_add_fusion = f32[30,30]{1,0:T(8,128)S(1)} fusion(f32[30,30]{1,0:T(8,128)} %param.22, f32[30]{0:T(128)S(1)} %compare_select_fusion), kind=kLoop, calls=%fused_computation.8 | loop fusion | flops 2700 | bytes 7320 | tf_op jit(solution)/shard_map/add | solution.py:443
  1.4 0.2 slice_reduce_fusion.column
  1.6 0.1 pad_maximum_fusion.1.mat_a
  1.7 0.8 %reduce-precision_convert_fusion = (bf16[56,56]{1,0:T(8,128)(2,1)S(1)}, bf16[56,56]{1,0:T(8,128)(2,1)S(1)}) fusion(f32[50,50]{1,0:T(8,128)} %param.23), kind=kLoop, calls=%fused_computation.1 | loop fusion | flops 12544 | bytes 22544 | tf_op jit(solution)/shard_map/convert
  2.5 0.1 pad_maximum_fusion.mat_o
  2.6 0.0 copy-start
  2.6 1.0 %copy-done = f32[1,16,48,128]{3,2,1,0:T(8,128)S(1)} copy-done((f32[1,16,48,128]{3,2,1,0:T(8,128)S(1)}, f32[1,16,48,128]{3,2,1,0:T(8,128)}, u32[]{:S(2)}) %copy-start) | copy-done | bytes 393240
  3.6 0.0 copy-start.1
  3.6 1.0 %copy-done.1 = f32[1,16,48,128]{3,2,1,0:T(8,128)S(1)} copy-done((f32[1,16,48,128]{3,2,1,0:T(8,128)S(1)}, f32[1,16,48,128]{3,2,1,0:T(8,128)}, u32[]{:S(2)}) %copy-start.1) | copy-done | bytes 393240
  4.6 0.0 copy-start.2
  4.6 0.9 %copy-done.2 = f32[24,1152]{1,0:T(8,128)S(1)} copy-done((f32[24,1152]{1,0:T(8,128)S(1)}, f32[24,1152]{1,0:T(8,128)}, u32[]{:S(2)}) %copy-start.2) | copy-done | bytes 110616
  5.5 0.0 copy-start.3
  5.5 0.9 %copy-done.3 = f32[24,1152]{1,0:T(8,128)S(1)} copy-done((f32[24,1152]{1,0:T(8,128)S(1)}, f32[24,1152]{1,0:T(8,128)}, u32[]{:S(2)}) %copy-start.3) | copy-done | bytes 110616
  6.4 0.0 copy-start.4
  6.4 0.8 %copy-done.4 = s32[8,1440]{1,0:T(8,128)S(1)} copy-done((s32[8,1440]{1,0:T(8,128)S(1)}, s32[8,1440]{1,0:T(8,128)}, u32[]{:S(2)}) %copy-start.4) | copy-done | bytes 46104
  7.2 0.0 copy-start.5
  7.2 0.8 %copy-done.5 = f32[8,1440]{1,0:T(8,128)S(1)} copy-done((f32[8,1440]{1,0:T(8,128)S(1)}, f32[8,1440]{1,0:T(8,128)}, u32[]{:S(2)}) %copy-start.5) | copy-done | bytes 46104
  8.0 0.0 copy-start.6
  8.0 0.7 %copy-done.6 = s32[1,16,48]{2,1,0:T(8,128)S(1)} copy-done((s32[1,16,48]{2,1,0:T(8,128)S(1)}, s32[1,16,48]{2,1,0:T(8,128)}, u32[]{:S(2)}) %copy-start.6) | copy-done | bytes 3096
  8.7 0.0 copy-start.7
  8.7 0.7 %copy-done.7 = s32[1,16,48]{2,1,0:T(8,128)S(1)} copy-done((s32[1,16,48]{2,1,0:T(8,128)S(1)}, s32[1,16,48]{2,1,0:T(8,128)}, u32[]{:S(2)}) %copy-start.7) | copy-done | bytes 3096
  9.4 0.0 copy-start.8
  9.4 0.7 %copy-done.8 = s32[1,16,48]{2,1,0:T(8,128)S(1)} copy-done((s32[1,16,48]{2,1,0:T(8,128)S(1)}, s32[1,16,48]{2,1,0:T(8,128)}, u32[]{:S(2)}) %copy-start.8) | copy-done | bytes 3096
  10.1 0.0 copy-start.9
  10.1 0.7 %copy-done.9 = s32[1,16,48]{2,1,0:T(8,128)S(1)} copy-done((s32[1,16,48]{2,1,0:T(8,128)S(1)}, s32[1,16,48]{2,1,0:T(8,128)}, u32[]{:S(2)}) %copy-start.9) | copy-done | bytes 3096
  10.7 0.0 copy-start.10
  10.7 0.7 %copy-done.10 = s32[1,16]{1,0:T(1,128)S(1)} copy-done((s32[1,16]{1,0:T(1,128)S(1)}, s32[1,16]{1,0:T(1,128)}, u32[]{:S(2)}) %copy-start.10) | copy-done | bytes 88
  11.4 0.0 copy-start.11
  11.4 0.7 %copy-done.11 = s32[1,16]{1,0:T(1,128)S(1)} copy-done((s32[1,16]{1,0:T(1,128)S(1)}, s32[1,16]{1,0:T(1,128)}, u32[]{:S(2)}) %copy-start.11) | copy-done | bytes 88
  12.1 30.4 %shard_map.175 = (f32[24,32,1152]{2,1,0:T(8,128)}, f32[8,56,1536]{2,1,0:T(8,128)}, f32[24,1152]{1,0:T(8,128)S(1)}, f32[24,1152]{1,0:T(8,128)S(1)}, f32[8,1536]{1,0:T(8,128)S(1)}) custom-call(f32[30,24,1152]{2,1,0:T(8,128)} %atmos.1, f32[50,8,1440]{2,1,0:T(8,128)} %water.1, f32[24,1152]{1,0:T(8,128)S(1)} %copy-done.2, s32[8,1440]{1,0:T(8,128)S(1)} %copy-done.4, ...), custom_call_target="tpu_custom_call" | custom-call | tf_op jit(solution)/shard_map/pallas_call | solution.py:452
  42.4 6.5 %shard_map.176 = (f32[30,24,1152]{2,1,0:T(8,128)}, f32[50,8,1440]{2,1,0:T(8,128)}, f32[24,1152]{1,0:T(8,128)}) custom-call(f32[24,32,1152]{2,1,0:T(8,128)} %get-tuple-element.8.u2, f32[24,1152]{1,0:T(8,128)S(1)} %get-tuple-element.9.g, f32[24,1152]{1,0:T(8,128)S(1)} %get-tuple-element.10.d, f32[30]{0:T(128)S(1)} %slice_reduce_fusion.column, ...), custom_call_target="tpu_custom_call" | custom-call | tf_op jit(solution)/shard_map/pallas_call | solution.py:509
  (2 shorter events, 0.0 us)
Async XLA Ops:
  2.6 1.0 %copy-start = (f32[1,16,48,128]{3,2,1,0:T(8,128)S(1)}, f32[1,16,48,128]{3,2,1,0:T(8,128)}, u32[]{:S(2)}) copy-start(f32[1,16,48,128]{3,2,1,0:T(8,128)} %f_wgt.1) | copy-start | bytes 1179652
  3.6 1.0 %copy-start.1 = (f32[1,16,48,128]{3,2,1,0:T(8,128)S(1)}, f32[1,16,48,128]{3,2,1,0:T(8,128)}, u32[]{:S(2)}) copy-start(f32[1,16,48,128]{3,2,1,0:T(8,128)} %w_wgt.1) | copy-start | bytes 1179652
  4.6 0.9 %copy-start.2 = (f32[24,1152]{1,0:T(8,128)S(1)}, f32[24,1152]{1,0:T(8,128)}, u32[]{:S(2)}) copy-start(f32[24,1152]{1,0:T(8,128)} %flux.1) | copy-start | bytes 331780
  5.5 0.9 %copy-start.3 = (f32[24,1152]{1,0:T(8,128)S(1)}, f32[24,1152]{1,0:T(8,128)}, u32[]{:S(2)}) copy-start(f32[24,1152]{1,0:T(8,128)} %kap_a.1) | copy-start | bytes 331780
  6.4 0.8 %copy-start.4 = (s32[8,1440]{1,0:T(8,128)S(1)}, s32[8,1440]{1,0:T(8,128)}, u32[]{:S(2)}) copy-start(s32[8,1440]{1,0:T(8,128)} %mask.1) | copy-start | bytes 138244
  7.2 0.8 %copy-start.5 = (f32[8,1440]{1,0:T(8,128)S(1)}, f32[8,1440]{1,0:T(8,128)}, u32[]{:S(2)}) copy-start(f32[8,1440]{1,0:T(8,128)} %kap_o.1) | copy-start | bytes 138244
  8.0 0.7 %copy-start.6 = (s32[1,16,48]{2,1,0:T(8,128)S(1)}, s32[1,16,48]{2,1,0:T(8,128)}, u32[]{:S(2)}) copy-start(s32[1,16,48]{2,1,0:T(8,128)} %f_src.1) | copy-start | bytes 9220
  8.7 0.7 %copy-start.7 = (s32[1,16,48]{2,1,0:T(8,128)S(1)}, s32[1,16,48]{2,1,0:T(8,128)}, u32[]{:S(2)}) copy-start(s32[1,16,48]{2,1,0:T(8,128)} %f_tgt.1) | copy-start | bytes 9220
  9.4 0.7 %copy-start.8 = (s32[1,16,48]{2,1,0:T(8,128)S(1)}, s32[1,16,48]{2,1,0:T(8,128)}, u32[]{:S(2)}) copy-start(s32[1,16,48]{2,1,0:T(8,128)} %w_src.1) | copy-start | bytes 9220
  10.1 0.7 %copy-start.9 = (s32[1,16,48]{2,1,0:T(8,128)S(1)}, s32[1,16,48]{2,1,0:T(8,128)}, u32[]{:S(2)}) copy-start(s32[1,16,48]{2,1,0:T(8,128)} %w_tgt.1) | copy-start | bytes 9220
  10.7 0.7 %copy-start.10 = (s32[1,16]{1,0:T(1,128)S(1)}, s32[1,16]{1,0:T(1,128)}, u32[]{:S(2)}) copy-start(s32[1,16]{1,0:T(1,128)} %f_cnt.1) | copy-start | bytes 196
  11.4 0.7 %copy-start.11 = (s32[1,16]{1,0:T(1,128)S(1)}, s32[1,16]{1,0:T(1,128)}, u32[]{:S(2)}) copy-start(s32[1,16]{1,0:T(1,128)} %w_cnt.1) | copy-start | bytes 196

commit v2 on v1

--- a/solution.py
+++ b/solution.py
@@ -11,7 +11,7 @@
 ENTRIES = 2
 AIR_EXCHANGER = 0.3
 COUPLE_OCEAN = 0.5
-VMEM_BYTES = 52 * 1024 * 1024
+VMEM_BYTES = 60 * 1024 * 1024
 
 
 def round_up(value, unit):
@@ -36,13 +36,15 @@
 
 def exchange_kernel(
     dims,
-    atmos, water, flux, mask, kap_a, kap_o, mat_a, mat_o,
-    f_src, f_tgt, f_cnt, f_wgt, w_src, w_tgt, w_cnt, w_wgt,
+    atmos, water, flux_in, mask_in, kap_a_in, kap_o_in, op_a_in, op_o_in,
+    f_src_in, f_tgt_in, f_cnt_in, f_wgt, w_src_in, w_tgt_in, w_cnt_in, w_wgt,
     u2_out, o2_out, g_out, d_out, fl_out,
+    flux, mask, kap_a, kap_o, op_a, op_o, f_src, f_tgt, f_cnt, w_src, w_tgt, w_cnt,
+    wide_a, wide_o, mat_a, mat_o,
     in_a, u, u1, u2, in_o, o, o2, surf,
     f_blocks, w_blocks, f_send, w_send, f_recv, w_recv, f_wbuf, w_wbuf,
     eff, f_terms, w_terms, r_a, r_o, t_o, r_halo, g_rows, lanes_o, kap_rows,
-    dma, f_ss, f_rs, w_ss, w_rs, h_ss, h_rs,
+    dma, small, f_ss, f_rs, w_ss, w_rs, h_ss, h_rs,
 ):
     n, la, ya, xa, lo, yo, xo, cap, nf, nw = dims
     lap, lop = round_up(la + 1, 8), round_up(lo, 8)
@@ -62,8 +64,20 @@
     for q in range(1, nw):
         pl.semaphore_signal(barrier, inc=1, device_id={"tiles": source_of(q)})
 
+    small_copies = [
+        pltpu.make_async_copy(src, dst, small.at[k])
+        for k, (src, dst) in enumerate(
+            (
+                (mask_in, mask), (w_src_in, w_src), (flux_in, flux), (f_src_in, f_src),
+                (kap_a_in, kap_a), (kap_o_in, kap_o), (op_a_in, op_a), (op_o_in, op_o),
+                (f_tgt_in, f_tgt), (w_tgt_in, w_tgt), (f_cnt_in, f_cnt), (w_cnt_in, w_cnt),
+            )
+        )
+    ]
     surf_copy = pltpu.make_async_copy(water.at[0], surf, dma.at[0])
     surf_copy.start()
+    for c in small_copies:
+        c.start()
     groups = ya // 8
     air_copies = [
         pltpu.make_async_copy(atmos.at[:, pl.ds(8 * i, 8), :], in_a.at[i], dma.at[1 + i])
@@ -86,9 +100,11 @@
     for c in wgt_copies:
         c.start()
 
+    surf_copy.wait()
+    for c in small_copies[:4]:
+        c.wait()
     for j in range(ja):
         f_blocks[pl.ds(j, ya, stride=ja), :] = flux[:, j * LANES : (j + 1) * LANES]
-    surf_copy.wait()
     sea2 = mask[...].astype(jnp.float32)
     lanes_o[...] = jnp.zeros_like(lanes_o)
     lanes_o[:, 0:xo] = surf[...] * sea2
@@ -138,6 +154,21 @@
         if q in f_copies:
             f_copies[q].start()
 
+    for c in small_copies[4:]:
+        c.wait()
+    step = op_a[...]
+    row = lax.broadcasted_iota(jnp.int32, (la, la), 0)
+    keep = jnp.where(row == la - 1, 1.0 - AIR_EXCHANGER, 1.0)
+    step = step + jnp.where(row == lane_iota((la, la)), keep, 0.0)
+    for wide, out, matrix, size in ((wide_a, mat_a, step, lap), (wide_o, mat_o, op_o[...], lop)):
+        side = matrix.shape[0]
+        high = matrix.astype(jnp.bfloat16).astype(jnp.float32)
+        wide[...] = jnp.zeros_like(wide)
+        wide[0:side, 0:side] = high
+        wide[0:side, size : size + side] = high
+        wide[0:side, 2 * size : 2 * size + side] = matrix - high
+        out[...] = wide[...].astype(jnp.bfloat16)
+
     kap_rows[...] = jnp.zeros_like(kap_rows)
 
     def turn_air(i):
@@ -221,7 +252,18 @@
     def first_step(y):
         air_step(u1, (y + 1, y + 2), u, y + 2)
 
-    lax.fori_loop(1, ya - 1, lambda y, c: (first_step(y), c)[1], 0)
+    def rows_loop(start, stop, unroll, row_step):
+        def body(k, carry):
+            for r in range(unroll):
+                row_step(start + k * unroll + r)
+            return carry
+
+        whole = (stop - start) // unroll
+        lax.fori_loop(0, whole, body, 0)
+        for y in range(start + whole * unroll, stop):
+            row_step(y)
+
+    rows_loop(1, ya - 1, 4, first_step)
 
     lanes_o[...] = jnp.zeros_like(lanes_o)
     lanes_o[:, 0:xo] = sea2
@@ -234,7 +276,7 @@
         beside = o[y] + o[y + 2] + pltpu.roll(c, 1, 1) + pltpu.roll(c, xop - 1, 1)
         o2[y] = c + wet * (kap * (beside - 4.0 * c) + split_product(mat_o[...], c))
 
-    lax.fori_loop(1, yo - 1, lambda y, c: (sea_step(y), c)[1], 0)
+    rows_loop(1, yo - 1, 2, sea_step)
 
     @pl.when(has_prev)
     def _():
@@ -255,19 +297,12 @@
     for y in (-1, 0, ya - 1, ya):
         first_step(y)
 
-    u2_copies = []
+    out_copies = []
     for i in range(groups):
-        lax.fori_loop(
-            8 * i,
-            8 * i + 8,
-            lambda y, c: (air_step(u2, (y, y + 2), u1, y + 1), c)[1],
-            0,
-        )
-        copy = pltpu.make_async_copy(
-            u2.at[pl.ds(8 * i, 8)], u2_out.at[pl.ds(8 * i, 8)], dma.at[1 + i]
-        )
-        copy.start()
-        u2_copies.append(copy)
+        rows_loop(8 * i, 8 * i + 8, 4, lambda y: air_step(u2, (y, y + 2), u1, y + 1))
+        rows = pl.ds(8 * i, 8)
+        out_copies.append(pltpu.make_async_copy(u2.at[rows], u2_out.at[rows], dma.at[1 + i]))
+        out_copies[-1].start()
 
     @pl.when(has_prev)
     def _():
@@ -287,8 +322,8 @@
 
     sea_step(0)
     sea_step(yo - 1)
-    o2_copy = pltpu.make_async_copy(o2, o2_out, dma.at[0])
-    o2_copy.start()
+    out_copies.append(pltpu.make_async_copy(o2, o2_out, dma.at[0]))
+    out_copies[-1].start()
 
     for c in wgt_copies:
         c.wait()
@@ -365,9 +400,8 @@
     )
     d_out[...] = kap_a[...] * (beside - 4.0 * g) + g
 
-    for c in u2_copies:
+    for c in out_copies:
         c.wait()
-    o2_copy.wait()
     for q in range(1, nw):
         w_copies[q].wait_send()
     for q in range(1, nf):
@@ -386,26 +420,63 @@
         blk_down.wait_send()
 
 
-def finish_kernel(la, lo, u2, g, d, column, o2, fl, air, sea, energy):
-    turned = jnp.swapaxes(u2[...], 0, 1)
-    warm = g[...]
-    for k in range(la):
-        level = turned[k] + column[k] * warm
-        if k == la - 1:
-            level = level + d[...]
-            energy[...] = warm - AIR_EXCHANGER * level
-        air[k] = level
-    turned = jnp.swapaxes(o2[...], 0, 1)
-    sea[0] = turned[0] + fl[...]
-    for k in range(1, lo):
-        sea[k] = turned[k]
-
-
-def parts_of(matrix, rows):
-    padded = jnp.pad(matrix, ((0, rows - matrix.shape[0]), (0, rows - matrix.shape[1])))
-    high = lax.reduce_precision(padded, 8, 7)
-    low = padded - high
-    return jnp.concatenate([high, high, low], axis=1).astype(jnp.bfloat16)
+def finish_kernel(
+    dims,
+    u2_in, g_in, d_in, op_a_in, o2_in, fl_in, air_out, sea_out, energy,
+    u2, g, d, op_a, o2, fl, air, sea, in_sem, sem,
+):
+    n, la, ya, xa, lo, yo, xo, cap, nf, nw = dims
+    groups = ya // 8
+    arrivals = [
+        pltpu.make_async_copy(src, dst, in_sem.at[groups + k])
+        for k, (src, dst) in enumerate(
+            ((g_in, g), (d_in, d), (op_a_in, op_a), (fl_in, fl), (o2_in, o2))
+        )
+    ]
+    levels = [
+        pltpu.make_async_copy(u2_in.at[pl.ds(8 * i, 8)], u2.at[pl.ds(8 * i, 8)], in_sem.at[i])
+        for i in range(groups)
+    ]
+    for c in arrivals[:3] + levels + arrivals[3:]:
+        c.start()
+    for c in arrivals[:3]:
+        c.wait()
+    copies = []
+
+    def send(src, dst):
+        copies.append(pltpu.make_async_copy(src, dst, sem.at[len(copies)]))
+        copies[-1].start()
+
+    for i in range(groups):
+        rows = pl.ds(8 * i, 8)
+        levels[i].wait()
+        for j in range(xa // LANES):
+            cut = pl.ds(j * LANES, LANES)
+            turned = jnp.swapaxes(u2[rows, :, cut], 0, 1)
+            warm = g[rows, cut]
+            for k in range(la):
+                level = turned[k] + op_a[k : k + 1, la - 1 : la] * warm
+                if k == la - 1:
+                    level = level + (d[rows, cut] + (1.0 - AIR_EXCHANGER) * warm)
+                    energy[rows, cut] = warm - AIR_EXCHANGER * level
+                air[i, k, :, cut] = level
+        send(air.at[i], air_out.at[:, rows, :])
+    for c in arrivals[3:]:
+        c.wait()
+    for j in range(-(-xo // LANES)):
+        width = min(LANES, xo - j * LANES)
+        cut = pl.ds(j * LANES, width)
+        turned = jnp.swapaxes(o2[:, :, cut], 0, 1)
+        sea[0, :, cut] = turned[0] + fl[:, cut]
+        sea[1:lo, :, cut] = turned[1:lo]
+        edge = (j + 1) * LANES
+        if edge % 512 == 0 and edge < xo:
+            part = pl.ds(edge - 512, 512)
+            send(sea.at[:, :, part], sea_out.at[:, :, part])
+    rest = (xo // 512) * 512
+    send(sea.at[:, :, pl.ds(rest, xo - rest)], sea_out.at[:, :, pl.ds(rest, xo - rest)])
+    for c in copies:
+        c.wait()
 
 
 def shards(
@@ -438,16 +509,9 @@
     xop = round_up(xo, LANES)
     jo = xop // LANES
 
-    level = jnp.arange(la)
-    diagonal = jnp.where(level == la - 1, 1.0 - AIR_EXCHANGER, 1.0).astype(jnp.float32)
-    step_matrix = air_vertical_operator + jnp.diag(diagonal)
-    mat_a = parts_of(step_matrix, lap)
-    mat_o = parts_of(ocean_column, lop)
-
     f32 = jnp.float32
     vm = pl.BlockSpec(memory_space=pltpu.VMEM)
-    sm = pl.BlockSpec(memory_space=pltpu.SMEM)
-    hb = pl.BlockSpec(memory_space=pl.ANY)
+    hb = pl.BlockSpec(memory_space=pltpu.HBM)
     S = jax.ShapeDtypeStruct
     u2, o2, g, d, fl = pl.pallas_call(
         functools.partial(exchange_kernel, dims),
@@ -458,9 +522,25 @@
             S((ya, xa), f32),
             S((yo, xop), f32),
         ),
-        in_specs=[hb, hb, vm, vm, vm, vm, vm, vm, sm, vm, sm, hb, sm, vm, sm, hb],
+        in_specs=[hb] * 16,
         out_specs=(hb, hb, vm, vm, vm),
         scratch_shapes=[
+            pltpu.VMEM((ya, xa), f32),
+            pltpu.VMEM((yo, xo), jnp.int32),
+            pltpu.VMEM((ya, xa), f32),
+            pltpu.VMEM((yo, xo), f32),
+            pltpu.VMEM((la, la), f32),
+            pltpu.VMEM((lo, lo), f32),
+            pltpu.SMEM((1, tiles, cap), jnp.int32),
+            pltpu.VMEM((1, tiles, cap), jnp.int32),
+            pltpu.SMEM((1, tiles), jnp.int32),
+            pltpu.SMEM((1, tiles, cap), jnp.int32),
+            pltpu.VMEM((1, tiles, cap), jnp.int32),
+            pltpu.SMEM((1, tiles), jnp.int32),
+            pltpu.VMEM((lap, 3 * lap), f32),
+            pltpu.VMEM((lop, 3 * lop), f32),
+            pltpu.VMEM((lap, 3 * lap), jnp.bfloat16),
+            pltpu.VMEM((lop, 3 * lop), jnp.bfloat16),
             pltpu.VMEM((ya // 8, la, 8, xa), f32),
             pltpu.VMEM((ya + 4, lap, xa), f32),
             pltpu.VMEM((ya + 2, lap, xa), f32),
@@ -488,6 +568,7 @@
             pltpu.VMEM((yo, xop), f32),
             pltpu.VMEM((yo, xop), f32),
             pltpu.SemaphoreType.DMA((2 + ya // 8 + nw + nf,)),
+            pltpu.SemaphoreType.DMA((12,)),
             pltpu.SemaphoreType.DMA((nf - 1,)),
             pltpu.SemaphoreType.DMA((nf - 1,)),
             pltpu.SemaphoreType.DMA((nw - 1,)),
@@ -499,32 +580,30 @@
             collective_id=0, has_side_effects=True, vmem_limit_bytes=VMEM_BYTES
         ),
     )(
-        atmos, water_anomaly, atm_flux, ocean_mask, air_mixing_numbers, ocean_kappa, mat_a, mat_o,
+        atmos, water_anomaly, atm_flux, ocean_mask, air_mixing_numbers, ocean_kappa, air_vertical_operator, ocean_column,
         a2o_source, a2o_target, a2o_count, a2o_weight,
         water_air_provider, water_air_receiver, water_air_live_tally, water_air_overlay_share,
     )
 
-    steps = ya // 8
-    cut = round_up(-(-xop // steps), LANES)
     return pl.pallas_call(
-        functools.partial(finish_kernel, la, lo),
-        grid=(steps,),
+        functools.partial(finish_kernel, dims),
         out_shape=(S((la, ya, xa), f32), S((lo, yo, xo), f32), S((ya, xa), f32)),
-        in_specs=[
-            pl.BlockSpec((8, lap, xa), lambda i: (i, 0, 0)),
-            pl.BlockSpec((8, xa), lambda i: (i, 0)),
-            pl.BlockSpec((8, xa), lambda i: (i, 0)),
-            pl.BlockSpec(memory_space=pltpu.SMEM),
-            pl.BlockSpec((yo, lop, cut), lambda i: (0, 0, i)),
-            pl.BlockSpec((yo, cut), lambda i: (0, i)),
+        in_specs=[hb] * 6,
+        out_specs=(hb, hb, vm),
+        scratch_shapes=[
+            pltpu.VMEM((ya, lap, xa), f32),
+            pltpu.VMEM((ya, xa), f32),
+            pltpu.VMEM((ya, xa), f32),
+            pltpu.VMEM((la, la), f32),
+            pltpu.VMEM((yo, lop, xop), f32),
+            pltpu.VMEM((yo, xop), f32),
+            pltpu.VMEM((ya // 8, la, 8, xa), f32),
+            pltpu.VMEM((lo, yo, xo), f32),
+            pltpu.SemaphoreType.DMA((ya // 8 + 5,)),
+            pltpu.SemaphoreType.DMA((ya // 8 + xo // 512 + 1,)),
         ],
-        out_specs=(
-            pl.BlockSpec((la, 8, xa), lambda i: (0, i, 0)),
-            pl.BlockSpec((lo, yo, cut), lambda i: (0, 0, i)),
-            pl.BlockSpec((8, xa), lambda i: (i, 0)),
-        ),
         compiler_params=pltpu.CompilerParams(vmem_limit_bytes=VMEM_BYTES),
-    )(u2, g, d, step_matrix[:, la - 1], o2, fl)
+    )(u2, g, d, air_vertical_operator, o2, fl)
 
 
 def solution(mesh):

time: 49.7 us -> 36.1 us (0.73); the launches traced: 48.9 us -> 35.9 us
  local copies, waits for them, and re-layouts: 9.65 us -> 0 us
  other arithmetic: 1.73 us -> 0 us
  Pallas kernels: 36.9 us -> 35.3 us
    unnamed x24 -> x0, local copies, waits for them, and re-layouts: 9.47 us -> none
    pallas_call x1, Pallas kernels: 6.51 us -> 5.59 us  [shards(): pl.pallas_call(functools.partial(finish_kernel, dims), out_shape=(S((la,...]
    add x1 -> x0, other arithmetic: 0.79 us -> none  [shards(): step_matrix = air_vertical_operator + jnp.diag(diagonal)]
    another operation x2 -> x0, other arithmetic: 0.77 us -> none
    pallas_call x1, Pallas kernels: 30.4 us -> 29.7 us  [shards(): pl.pallas_call(functools.partial(exchange_kernel, dims), out_shape=(S((ya...]
where the time goes in v2:
time: 36.1 us; the launch traced here: 35.9 us
  Pallas kernels  35.3 us (98%)
  between operations  0.64 us (2%)
    pallas_call x1, Pallas kernels, shards(): pl.pallas_call(functools.partial(exchange_kernel, dims), out_shape=(S((ya...  29.7 us
    pallas_call x1, Pallas kernels, shards(): pl.pallas_call(functools.partial(finish_kernel, dims), out_shape=(S((la,...  5.59 us

profile of v2, /device:TPU:1, one launch (start us, length us, event | category | flops | bytes accessed | tf_op | source)
XLA Modules:
  0.0 35.9 jit_solution(8741949375226856886)
XLA Ops:
  0.6 29.7 %shard_map.175 = (f32[24,32,1152]{2,1,0:T(8,128)}, f32[8,56,1536]{2,1,0:T(8,128)}, f32[24,1152]{1,0:T(8,128)}, f32[24,1152]{1,0:T(8,128)}, f32[8,1536]{1,0:T(8,128)}) custom-call(f32[30,24,1152]{2,1,0:T(8,128)} %atmos.1, f32[50,8,1440]{2,1,0:T(8,128)} %water.1, f32[24,1152]{1,0:T(8,128)} %flux_in.1, s32[8,1440]{1,0:T(8,128)} %mask_in.1, ...), custom_call_target="tpu_custom_call" | custom-call | tf_op jit(solution)/shard_map/pallas_call | solution.py:516
  30.3 5.6 %shard_map.176 = (f32[30,24,1152]{2,1,0:T(8,128)}, f32[50,8,1440]{2,1,0:T(8,128)}, f32[24,1152]{1,0:T(8,128)}) custom-call(f32[24,32,1152]{2,1,0:T(8,128)} %get-tuple-element.8.u2_in, f32[24,1152]{1,0:T(8,128)} %get-tuple-element.9.g_in, f32[24,1152]{1,0:T(8,128)} %get-tuple-element.10.d_in, f32[30,30]{1,0:T(8,128)} %op_a_in.3, ...), custom_call_target="tpu_custom_call" | custom-call | tf_op jit(solution)/shard_map/pallas_call | solution.py:588

commit v3 on v2

--- a/solution.py
+++ b/solution.py
@@ -100,6 +100,54 @@
     for c in wgt_copies:
         c.start()
 
+    kap_rows[...] = jnp.zeros_like(kap_rows)
+
+    def turn_air(i):
+        air_copies[i].wait()
+        for j in range(ja):
+            cut = pl.ds(j * LANES, LANES)
+            u[pl.ds(2 + 8 * i, 8), 0:la, cut] = jnp.swapaxes(in_a[i, :, :, cut], 0, 1)
+        for r in range(8):
+            u[2 + 8 * i + r, la : la + 1, :] = kap_a[8 * i + r : 8 * i + r + 1, :]
+            if lap > la + 1:
+                u[2 + 8 * i + r, la + 1 : lap, :] = jnp.zeros((lap - la - 1, xa), jnp.float32)
+
+    up, down = lax.rem(me + 1, n), lax.rem(me + n - 1, n)
+
+    def to_next(k, src, dst):
+        return pltpu.make_async_remote_copy(
+            src_ref=src, dst_ref=dst, send_sem=h_ss.at[k], recv_sem=h_rs.at[k],
+            device_id={"tiles": up},
+        )
+
+    def to_prev(k, src, dst):
+        return pltpu.make_async_remote_copy(
+            src_ref=src, dst_ref=dst, send_sem=h_ss.at[k], recv_sem=h_rs.at[k],
+            device_id={"tiles": down},
+        )
+
+    has_next, has_prev = me < n - 1, me > 0
+    air_up = to_next(0, u.at[pl.ds(ya, 2)], u.at[pl.ds(0, 2)])
+    air_down = to_prev(1, u.at[pl.ds(2, 2)], u.at[pl.ds(ya + 2, 2)])
+    sea_up = to_next(2, o.at[yo], o.at[0])
+    sea_down = to_prev(3, o.at[1], o.at[yo + 1])
+    blk_up = to_next(4, r_a.at[pl.ds(ya * ja - 16, 16)], r_halo.at[0])
+    blk_down = to_prev(5, r_a.at[pl.ds(0, 16)], r_halo.at[1])
+
+    small_copies[4].wait()
+    pl.semaphore_wait(barrier, nw - 1)
+    turn_air(0)
+
+    @pl.when(has_prev)
+    def _():
+        air_down.start()
+
+    turn_air(groups - 1)
+
+    @pl.when(has_next)
+    def _():
+        air_up.start()
+
     surf_copy.wait()
     for c in small_copies[:4]:
         c.wait()
@@ -137,7 +185,6 @@
     for q in range(nf):
         gather(f_recv.at[0] if q == 0 else f_send.at[q - 1], f_blocks, f_src, dest_of(q))
 
-    pl.semaphore_wait(barrier, nw - 1)
     w_copies, f_copies = {}, {}
     for q in range(1, nw):
         w_copies[q] = pltpu.make_async_remote_copy(
@@ -153,67 +200,6 @@
         w_copies[q].start()
         if q in f_copies:
             f_copies[q].start()
-
-    for c in small_copies[4:]:
-        c.wait()
-    step = op_a[...]
-    row = lax.broadcasted_iota(jnp.int32, (la, la), 0)
-    keep = jnp.where(row == la - 1, 1.0 - AIR_EXCHANGER, 1.0)
-    step = step + jnp.where(row == lane_iota((la, la)), keep, 0.0)
-    for wide, out, matrix, size in ((wide_a, mat_a, step, lap), (wide_o, mat_o, op_o[...], lop)):
-        side = matrix.shape[0]
-        high = matrix.astype(jnp.bfloat16).astype(jnp.float32)
-        wide[...] = jnp.zeros_like(wide)
-        wide[0:side, 0:side] = high
-        wide[0:side, size : size + side] = high
-        wide[0:side, 2 * size : 2 * size + side] = matrix - high
-        out[...] = wide[...].astype(jnp.bfloat16)
-
-    kap_rows[...] = jnp.zeros_like(kap_rows)
-
-    def turn_air(i):
-        air_copies[i].wait()
-        for j in range(ja):
-            cut = pl.ds(j * LANES, LANES)
-            u[pl.ds(2 + 8 * i, 8), 0:la, cut] = jnp.swapaxes(in_a[i, :, :, cut], 0, 1)
-        for r in range(8):
-            u[2 + 8 * i + r, la : la + 1, :] = kap_a[8 * i + r : 8 * i + r + 1, :]
-            if lap > la + 1:
-                u[2 + 8 * i + r, la + 1 : lap, :] = jnp.zeros((lap - la - 1, xa), jnp.float32)
-
-    up, down = lax.rem(me + 1, n), lax.rem(me + n - 1, n)
-
-    def to_next(k, src, dst):
-        return pltpu.make_async_remote_copy(
-            src_ref=src, dst_ref=dst, send_sem=h_ss.at[k], recv_sem=h_rs.at[k],
-            device_id={"tiles": up},
-        )
-
-    def to_prev(k, src, dst):
-        return pltpu.make_async_remote_copy(
-            src_ref=src, dst_ref=dst, send_sem=h_ss.at[k], recv_sem=h_rs.at[k],
-            device_id={"tiles": down},
-        )
-
-    has_next, has_prev = me < n - 1, me > 0
-    air_up = to_next(0, u.at[pl.ds(ya, 2)], u.at[pl.ds(0, 2)])
-    air_down = to_prev(1, u.at[pl.ds(2, 2)], u.at[pl.ds(ya + 2, 2)])
-    sea_up = to_next(2, o.at[yo], o.at[0])
-    sea_down = to_prev(3, o.at[1], o.at[yo + 1])
-    blk_up = to_next(4, r_a.at[pl.ds(ya * ja - 16, 16)], r_halo.at[0])
-    blk_down = to_prev(5, r_a.at[pl.ds(0, 16)], r_halo.at[1])
-
-    turn_air(0)
-
-    @pl.when(has_prev)
-    def _():
-        air_down.start()
-
-    turn_air(groups - 1)
-
-    @pl.when(has_next)
-    def _():
-        air_up.start()
 
     water_copy.wait()
     for j in range(jo):
@@ -240,6 +226,21 @@
     def _():
         sea_up.start()
 
+    for c in small_copies[5:]:
+        c.wait()
+    step = op_a[...]
+    row = lax.broadcasted_iota(jnp.int32, (la, la), 0)
+    keep = jnp.where(row == la - 1, 1.0 - AIR_EXCHANGER, 1.0)
+    step = step + jnp.where(row == lane_iota((la, la)), keep, 0.0)
+    for wide, out, matrix, size in ((wide_a, mat_a, step, lap), (wide_o, mat_o, op_o[...], lop)):
+        side = matrix.shape[0]
+        high = matrix.astype(jnp.bfloat16).astype(jnp.float32)
+        wide[...] = jnp.zeros_like(wide)
+        wide[0:side, 0:side] = high
+        wide[0:side, size : size + side] = high
+        wide[0:side, 2 * size : 2 * size + side] = matrix - high
+        out[...] = wide[...].astype(jnp.bfloat16)
+
     for i in range(1, groups - 1):
         turn_air(i)
 
@@ -263,7 +264,20 @@
         for y in range(start + whole * unroll, stop):
             row_step(y)
 
+    def second_step(y):
+        air_step(u2, (y, y + 2), u1, y + 1)
+
+    out_copies = []
+
+    def hand_out(i):
+        rows = pl.ds(8 * i, 8)
+        out_copies.append(pltpu.make_async_copy(u2.at[rows], u2_out.at[rows], dma.at[1 + i]))
+        out_copies[-1].start()
+
     rows_loop(1, ya - 1, 4, first_step)
+    rows_loop(2, ya - 2, 4, second_step)
+    for i in range(1, groups - 1):
+        hand_out(i)
 
     lanes_o[...] = jnp.zeros_like(lanes_o)
     lanes_o[:, 0:xo] = sea2
@@ -297,33 +311,10 @@
     for y in (-1, 0, ya - 1, ya):
         first_step(y)
 
-    out_copies = []
-    for i in range(groups):
-        rows_loop(8 * i, 8 * i + 8, 4, lambda y: air_step(u2, (y, y + 2), u1, y + 1))
-        rows = pl.ds(8 * i, 8)
-        out_copies.append(pltpu.make_async_copy(u2.at[rows], u2_out.at[rows], dma.at[1 + i]))
-        out_copies[-1].start()
-
-    @pl.when(has_prev)
-    def _():
-        sea_up.wait_recv()
-
-    @pl.when(jnp.logical_not(has_prev))
-    def _():
-        o[0] = jnp.zeros((lop, xop), jnp.float32)
-
-    @pl.when(has_next)
-    def _():
-        sea_down.wait_recv()
-
-    @pl.when(jnp.logical_not(has_next))
-    def _():
-        o[yo + 1] = jnp.zeros((lop, xop), jnp.float32)
-
-    sea_step(0)
-    sea_step(yo - 1)
-    out_copies.append(pltpu.make_async_copy(o2, o2_out, dma.at[0]))
-    out_copies[-1].start()
+    for y in (0, 1, ya - 2, ya - 1):
+        second_step(y)
+    hand_out(0)
+    hand_out(groups - 1)
 
     for c in wgt_copies:
         c.wait()
@@ -372,6 +363,27 @@
     for j in range(jo):
         cut = slice(j * LANES, (j + 1) * LANES)
         fl_out[:, cut] = t_o[pl.ds(j, yo, stride=jo), :] * lanes_o[:, cut]
+
+    @pl.when(has_prev)
+    def _():
+        sea_up.wait_recv()
+
+    @pl.when(jnp.logical_not(has_prev))
+    def _():
+        o[0] = jnp.zeros((lop, xop), jnp.float32)
+
+    @pl.when(has_next)
+    def _():
+        sea_down.wait_recv()
+
+    @pl.when(jnp.logical_not(has_next))
+    def _():
+        o[yo + 1] = jnp.zeros((lop, xop), jnp.float32)
+
+    sea_step(0)
+    sea_step(yo - 1)
+    out_copies.append(pltpu.make_async_copy(o2, o2_out, dma.at[0]))
+    out_copies[-1].start()
 
     for j in range(ja):
         g_rows[8 : 8 + ya, j * LANES : (j + 1) * LANES] = r_a[pl.ds(j, ya, stride=ja), :]

time: 36.1 us -> 33.6 us (0.931)
  the two profiles are of different devices: /device:TPU:1 before, /device:TPU:6 now
where the time goes in v3:
time: 33.6 us; the launch traced here: 33.4 us
  Pallas kernels  32.8 us (98%)
  between operations  0.64 us (2%)
    pallas_call x1, Pallas kernels, shards(): pl.pallas_call(functools.partial(exchange_kernel, dims), out_shape=(S((ya...  27.2 us
    pallas_call x1, Pallas kernels, shards(): pl.pallas_call(functools.partial(finish_kernel, dims), out_shape=(S((la,...  5.59 us

profile of v3, /device:TPU:6, one launch (start us, length us, event | category | flops | bytes accessed | tf_op | source)
XLA Modules:
  0.0 33.4 jit_solution(9782005689878813791)
XLA Ops:
  0.6 27.2 %shard_map.175 = (f32[24,32,1152]{2,1,0:T(8,128)}, f32[8,56,1536]{2,1,0:T(8,128)}, f32[24,1152]{1,0:T(8,128)}, f32[24,1152]{1,0:T(8,128)}, f32[8,1536]{1,0:T(8,128)}) custom-call(f32[30,24,1152]{2,1,0:T(8,128)} %atmos.1, f32[50,8,1440]{2,1,0:T(8,128)} %water.1, f32[24,1152]{1,0:T(8,128)} %flux_in.1, s32[8,1440]{1,0:T(8,128)} %mask_in.1, ...), custom_call_target="tpu_custom_call" | custom-call | tf_op jit(solution)/shard_map/pallas_call | solution.py:528
  27.8 5.6 %shard_map.176 = (f32[30,24,1152]{2,1,0:T(8,128)}, f32[50,8,1440]{2,1,0:T(8,128)}, f32[24,1152]{1,0:T(8,128)}) custom-call(f32[24,32,1152]{2,1,0:T(8,128)} %get-tuple-element.8.u2_in, f32[24,1152]{1,0:T(8,128)} %get-tuple-element.9.g_in, f32[24,1152]{1,0:T(8,128)} %get-tuple-element.10.d_in, f32[30,30]{1,0:T(8,128)} %op_a_in.3, ...), custom_call_target="tpu_custom_call" | custom-call | tf_op jit(solution)/shard_map/pallas_call | solution.py:600
